TPU v7x, 32 devices: a whole 2x2x4 slice. The times are simulated.
32 devices in a mesh: groups: 2 (over y), length: 4 (over z), sector: 2 (over x), pair: 2 (over core).
Axes of the slice: x: 2, y: 2, z: 4, core: 2. Of those that a mesh axis runs over, the one named last changes fastest.
Arguments:
- flag_kernels: bfloat16 [4, 8, 32, 25, 1024], P('length', ('groups', 'sector', 'pair')), parts along dimension 1, may hold values from -1.1953125 to 1.1953125
- flag_unary: bfloat16 [4, 8, 32, 8, 1024], P('length', ('groups', 'sector', 'pair')), parts along dimension 1, may hold values from -8 to 8
- flag_labels: int32 [4, 8, 32, 1024], P('length', ('groups', 'sector', 'pair')), parts along dimension 1, may hold values from 0 to 7
- flag_mask: int32 [4, 8, 32, 1024], P('length', ('groups', 'sector', 'pair')), parts along dimension 1, may hold values 0 or 1
- dest_list: int32 [4, 8, 32], P('length', ('groups', 'sector', 'pair')), parts along dimension 1, may hold values from -1 to 3, as said below
- slot_list: int32 [4, 8, 32], P('length', ('groups', 'sector', 'pair')), parts along dimension 1, may hold values from -1 to 15, as said below
- res_kernels: bfloat16 [4, 8, 8, 25, 1024], P('length', ('groups', 'sector', 'pair')), parts along dimension 1, may hold values from -1.1953125 to 1.1953125
- res_unary: bfloat16 [4, 8, 8, 8, 1024], P('length', ('groups', 'sector', 'pair')), parts along dimension 1, may hold values from -8 to 8
- res_labels: int32 [4, 8, 8, 1024], P('length', ('groups', 'sector', 'pair')), parts along dimension 1, may hold values from 0 to 7
- res_mask: int32 [4, 8, 8, 1024], P('length', ('groups', 'sector', 'pair')), parts along dimension 1, may hold values 0 or 1
Outputs:
- flag_grad: bfloat16 [4, 8, 32, 25, 1024], P('length', ('groups', 'sector', 'pair')), parts along dimension 1
- res_grad: bfloat16 [4, 8, 8, 25, 1024], P('length', ('groups', 'sector', 'pair')), parts along dimension 1
- helper_loss: float32 [4, 8, 16], P('length', ('groups', 'sector', 'pair')), parts along dimension 1
There are 2 independent parts, one for each index of `groups`. A program takes and returns all parts, laid end to end along the dimension named above; each array names one. Nothing has to cross between parts.
Inputs may be any that keep to these rules, and one draw needn't show every extreme that they name: `dest_list`: entry j of a device's list is -1 exactly when its slot j holds no flagged tile, and the -1 entries come after all others; at most 8 entries of one device name the same destination. `slot_list`: for each index along sector and pair, each pair of a destination along length and a slot 0 to 15 is named by exactly one entry of the lists of the devices along length; an entry is -1 exactly where dest_list is -1.
All inputs are finite; a program needn't handle non-finite values. No bound on the sum of `flag_mask` or of `res_mask` on one device may be relied on, other than what follows from the above.
Results may differ from a plain program's by a relative error of at most 0.001.
Values may be sent and summed in bfloat16 or wider, within the bound.
No kernel may reach another device: no remote copies, remote signals or barrier semaphores. Data moves between devices by JAX's collectives and lax.ppermute only.
A program may use at most 64 MiB of HBM per device.

v0:
```python
import jax
import jax.numpy as jnp
from jax import lax
from jax.sharding import PartitionSpec as P

CLASSES = 8
TILE = 32
ITERS = 3
RECV = 16


def normalize(logits):
    raised = jnp.exp(logits)
    return raised / jnp.sum(raised, axis=0, keepdims=True)


def message(field_values, tap_weights):
    tile_side = TILE
    pixels = tile_side * tile_side
    margin = 2 * tile_side + 2
    padded = jnp.pad(field_values, ((0, 0), (margin, margin)))
    column = jnp.arange(pixels) % tile_side
    summed = jnp.zeros_like(field_values)
    tap_index = 0
    for row_step in range(-2, 3):
        for col_step in range(-2, 3):
            offset = row_step * tile_side + col_step
            shifted = lax.slice_in_dim(padded, margin + offset, margin + offset + pixels, axis=1)
            inside = ((column + col_step >= 0) & (column + col_step < tile_side)).astype(
                jnp.float32
            )
            summed = summed + (tap_weights[tap_index] * inside)[None, :] * shifted
            tap_index += 1
    return summed


def tile_objective(tap_weights, unary_terms, labels, weights):
    unary_terms = unary_terms.astype(jnp.float32)
    beliefs = normalize(unary_terms)
    logits = unary_terms
    for sweep_index in range(ITERS):
        logits = unary_terms + message(beliefs, tap_weights)
        if sweep_index + 1 < ITERS:
            beliefs = normalize(logits)
    summed = jnp.log(jnp.sum(jnp.exp(logits), axis=0))
    chosen = jnp.sum(
        jnp.where(jnp.arange(CLASSES)[:, None] == labels[None, :], logits, 0.0), axis=0
    )
    return jnp.sum(weights * (summed - chosen))


def tile_work(tap_weights, unary_terms, labels, weights):
    total_value, gradient = jax.value_and_grad(tile_objective)(
        tap_weights.astype(jnp.float32), unary_terms, labels, weights
    )
    return (total_value / TILE, gradient.astype(jnp.bfloat16))


def batched(tap_weights, unary_terms, labels, weights, block_size):
    amount = tap_weights.shape[0]

    def compute_block(group_arrays):
        return jax.vmap(tile_work)(*group_arrays)

    shaped = tuple(
        (
            member.reshape((amount // block_size, block_size) + member.shape[1:])
            for member in (tap_weights, unary_terms, labels, weights)
        )
    )
    losses, slopes = lax.map(compute_block, shaped)
    return (losses.reshape(amount), slopes.reshape((amount,) + slopes.shape[2:]))


def on_device(
    flag_kernels,
    flag_unary,
    flag_labels,
    flag_mask,
    dest_list,
    slot_list,
    res_kernels,
    res_unary,
    res_labels,
    res_mask,
):
    resident_losses, resident_slopes = batched(
        res_kernels[0, 0], res_unary[0, 0], res_labels[0, 0], res_mask[0, 0].astype(jnp.float32), 4
    )
    tap_weights = flag_kernels[0, 0]
    unary_flag = flag_unary[0, 0]
    labels_flag = flag_labels[0, 0]
    mask_flag = flag_mask[0, 0]
    destinations = dest_list[0, 0]
    slot_names = slot_list[0, 0]
    length_count = lax.axis_size("length")
    flag_count = destinations.shape[0]
    capacity = flag_count // length_count
    slot_order = jnp.arange(flag_count, dtype=jnp.int32)
    is_listed = destinations >= 0
    earlier = (destinations[:, None] == destinations[None, :]) & (
        slot_order[None, :] < slot_order[:, None]
    )
    earlier_count = jnp.sum(earlier.astype(jnp.int32), axis=1)
    buffer_place = jnp.where(is_listed, destinations * capacity + earlier_count, -1)
    hit_table = buffer_place[None, :] == slot_order[:, None]
    filled = jnp.any(hit_table, axis=1)
    source = jnp.sum(jnp.where(hit_table, slot_order[None, :], 0), axis=1)
    note_slot = jnp.where(filled, jnp.take(slot_names, source), -1)
    recv_order = jnp.arange(RECV, dtype=jnp.int32)
    send_taps = jnp.take(tap_weights, source, axis=0)
    send_taps = jnp.where(filled[:, None, None], send_taps, jnp.zeros_like(send_taps))
    send_unary = jnp.take(unary_flag, source, axis=0)
    send_unary = jnp.where(filled[:, None, None], send_unary, jnp.zeros_like(send_unary))
    target_class = jnp.where(mask_flag == 1, labels_flag, CLASSES)
    send_target = jnp.where(
        filled[:, None], jnp.take(target_class, source, axis=0), CLASSES
    ).astype(jnp.bfloat16)
    got_taps, got_unary, got_target, got_slot = (
        lax.all_to_all(send_taps, "length", split_axis=0, concat_axis=0, tiled=True),
        lax.all_to_all(send_unary, "length", split_axis=0, concat_axis=0, tiled=True),
        lax.all_to_all(send_target, "length", split_axis=0, concat_axis=0, tiled=True),
        lax.all_to_all(
            note_slot.astype(jnp.bfloat16), "length", split_axis=0, concat_axis=0, tiled=True
        ),
    )
    got_names = got_slot.astype(jnp.int32)
    slot_match = got_names[None, :] == recv_order[:, None]
    picked = jnp.sum(jnp.where(slot_match, slot_order[None, :], 0), axis=1)
    work_target = jnp.take(got_target, picked, axis=0).astype(jnp.int32)
    losses, slopes = batched(
        jnp.take(got_taps, picked, axis=0),
        jnp.take(got_unary, picked, axis=0),
        jnp.minimum(work_target, CLASSES - 1),
        (work_target < CLASSES).astype(jnp.float32),
        4,
    )
    sent_back = jnp.take(slopes, jnp.clip(got_names, 0, RECV - 1), axis=0)
    sent_back = jnp.where((got_names >= 0)[:, None, None], sent_back, jnp.zeros_like(sent_back))
    returned = lax.all_to_all(sent_back, "length", split_axis=0, concat_axis=0, tiled=True)
    flag_slopes = jnp.take(returned, jnp.clip(buffer_place, 0, flag_count - 1), axis=0)
    flag_slopes = jnp.where(is_listed[:, None, None], flag_slopes, jnp.zeros_like(flag_slopes))
    return (flag_slopes[None, None], resident_slopes[None, None], losses[None, None])


def solution(mesh):
    in_specs = (
        P("length", ("groups", "sector", "pair"), None, None, None),
        P("length", ("groups", "sector", "pair"), None, None, None),
        P("length", ("groups", "sector", "pair"), None, None),
        P("length", ("groups", "sector", "pair"), None, None),
        P("length", ("groups", "sector", "pair"), None),
        P("length", ("groups", "sector", "pair"), None),
        P("length", ("groups", "sector", "pair"), None, None, None),
        P("length", ("groups", "sector", "pair"), None, None, None),
        P("length", ("groups", "sector", "pair"), None, None),
        P("length", ("groups", "sector", "pair"), None, None),
    )
    out_specs = (
        P("length", ("groups", "sector", "pair"), None, None, None),
        P("length", ("groups", "sector", "pair"), None, None, None),
        P("length", ("groups", "sector", "pair"), None),
    )
    return jax.shard_map(
        on_device, mesh=mesh, in_specs=in_specs, out_specs=out_specs, check_vma=False
    )
```

profile of v0, /device:TPU:0, one launch (start us, length us, event | category | flops | bytes accessed | tf_op | source)
XLA Modules:
  0.0 227.4 jit_solution(15727652166822579169)
XLA Ops:
  5.3 6.3 %all-to-all-start = ((bf16[4,8,1]{1,2,0:T(2,128)(2,1)}), bf16[4,8,1]{1,2,0:T(2,128)(2,1)S(1)}, u32[]{:S(2)}, u32[]{:S(2)}) async-start(bf16[4,8,1]{1,2,0:T(2,128)(2,1)} %copy.26), calls=%async_computation | async-start | bytes 4096 | tf_op jit(solution)/shard_map/all_to_all | solution.py:123
  14.7 2.4 %all-to-all-done = bf16[4,8,1]{1,2,0:T(2,128)(2,1)S(1)} async-done(((bf16[4,8,1]{1,2,0:T(2,128)(2,1)}), bf16[4,8,1]{1,2,0:T(2,128)(2,1)S(1)}, u32[]{:S(2)}, u32[]{:S(2)}) %all-to-all-start) | async-done | bytes 96 | tf_op jit(solution)/shard_map/all_to_all | solution.py:123
  17.1 3.3 %all-to-all-start.1 = ((bf16[4,8,1024]{2,1,0:T(8,128)(2,1)}), bf16[4,8,1024]{2,1,0:T(8,128)(2,1)S(1)}, u32[]{:S(2)}, u32[]{:S(2)}) async-start(bf16[4,8,1024]{2,1,0:T(8,128)(2,1)} %fusion.82), calls=%async_computation.1 | async-start | bytes 131072 | tf_op jit(solution)/shard_map/all_to_all | solution.py:122
  21.3 4.8 %all-to-all-done.1 = bf16[4,8,1024]{2,1,0:T(8,128)(2,1)S(1)} async-done(((bf16[4,8,1024]{2,1,0:T(8,128)(2,1)}), bf16[4,8,1024]{2,1,0:T(8,128)(2,1)S(1)}, u32[]{:S(2)}, u32[]{:S(2)}) %all-to-all-start.1) | async-done | bytes 65568 | tf_op jit(solution)/shard_map/all_to_all | solution.py:122
  26.1 3.5 %all-to-all-start.2 = ((bf16[32,8,1024]{2,1,0:T(8,128)(2,1)}), bf16[32,8,1024]{2,1,0:T(8,128)(2,1)S(1)}, u32[]{:S(2)}, u32[]{:S(2)}) async-start(bf16[32,8,1024]{2,1,0:T(8,128)(2,1)} %select_select_fusion.3), calls=%async_computation.2 | async-start | bytes 1048576 | tf_op jit(solution)/shard_map/all_to_all | solution.py:121
  29.5 2.4 %copy.139 = bf16[1,1,32,25,1024]{4,3,2,1,0:T(8,128)(2,1)S(1)} copy(bf16[1,1,32,25,1024]{4,2,3,1,0:T(8,128)(2,1)} %param.16) | data formatting | bytes 3276800 | tf_op args[0]
  31.9 2.0 gather_fusion.7
  33.9 3.2 %select_select_fusion.1 = bf16[32,25,1024]{2,1,0:T(8,128)(2,1)} fusion(bf16[32,25,1024]{2,1,0:T(8,128)(2,1)} %gather_fusion.7, pred[32]{0:T(512)(128)(4,1)S(1)} %compare_and_fusion.1, pred[32]{0:T(512)(128)(4,1)S(1)} %fusion.84), kind=kLoop, calls=%fused_computation.812 | loop fusion | flops 1638400 | bytes 3276864 | tf_op jit(solution)/shard_map/jit(_where)/select_n | solution.py:112
  37.2 4.6 %all-to-all-done.2 = bf16[32,8,1024]{2,1,0:T(8,128)(2,1)S(1)} async-done(((bf16[32,8,1024]{2,1,0:T(8,128)(2,1)}), bf16[32,8,1024]{2,1,0:T(8,128)(2,1)S(1)}, u32[]{:S(2)}, u32[]{:S(2)}) %all-to-all-start.2) | async-done | bytes 524320 | tf_op jit(solution)/shard_map/all_to_all | solution.py:121
  41.8 4.4 %all-to-all-start.3 = ((bf16[32,25,1024]{2,1,0:T(8,128)(2,1)}), bf16[32,25,1024]{2,1,0:T(8,128)(2,1)}, u32[]{:S(2)}, u32[]{:S(2)}) async-start(bf16[32,25,1024]{2,1,0:T(8,128)(2,1)} %select_select_fusion.1), calls=%async_computation.3 | async-start | bytes 4194304 | tf_op jit(solution)/shard_map/all_to_all | solution.py:120
  49.7 41.6 %all-to-all-done.3 = bf16[32,25,1024]{2,1,0:T(8,128)(2,1)} async-done(((bf16[32,25,1024]{2,1,0:T(8,128)(2,1)}), bf16[32,25,1024]{2,1,0:T(8,128)(2,1)}, u32[]{:S(2)}, u32[]{:S(2)}) %all-to-all-start.3) | async-done | bytes 1638432 | tf_op jit(solution)/shard_map/all_to_all | solution.py:120
  91.3 2.2 gather_fusion.5
  93.7 73.1 %while.26 = (s32[]{:T(128)}, f32[4,4]{1,0:T(4,128)}, bf16[4,4,25,1024]{3,2,1,0:T(8,128)(2,1)}, f32[4,4,1024]{2,1,0:T(4,128)}, bf16[4,4,8,1024]{3,2,1,0:T(8,128)(...) while((s32[]{:T(128)}, f32[4,4]{1,0:T(4,128)}, ...), condition=%wide.region_88.90_spmd, body=%wide.region_4.89_spmd.sunk | while | flops 22141448 | bytes 28793544 | solution.py:71
  107.4 3.4 %bitcast_dynamic-update-slice_fusion.4 = bf16[4,4,25,1024]{3,2,1,0:T(8,128)(2,1)} fusion(bf16[4,4,25,1024]{3,2,1,0:T(8,128)(2,1)} %get-tuple-element.1930, s32[]{:T(128)} %get-tuple-element.1928, f32[4,1,1024]{2,1,0:T(1,128)S(1)} %get-tuple-element.1514, f32[4,1,1024]{2,1,0:T(1,128)S(1)} %get-tuple-element.1530, ...), kind=kLoop, calls=%fused_computation.82.clone.1 | loop fusion | flops 7680000 | bytes 1491456 | tf_op jit(solution)/shard_map/while/body/jit(dynamic_update_index_in_dim)/dynamic_update_slice | solution.py:71
  125.6 3.4 %bitcast_dynamic-update-slice_fusion.4 = bf16[4,4,25,1024]{3,2,1,0:T(8,128)(2,1)} fusion(bf16[4,4,25,1024]{3,2,1,0:T(8,128)(2,1)} %get-tuple-element.1930, s32[]{:T(128)} %get-tuple-element.1928, f32[4,1,1024]{2,1,0:T(1,128)S(1)} %get-tuple-element.1514, f32[4,1,1024]{2,1,0:T(1,128)S(1)} %get-tuple-element.1530, ...), kind=kLoop, calls=%fused_computation.82.clone.1 | loop fusion | flops 7680000 | bytes 1491456 | tf_op jit(solution)/shard_map/while/body/jit(dynamic_update_index_in_dim)/dynamic_update_slice | solution.py:71
  143.9 3.4 %bitcast_dynamic-update-slice_fusion.4 = bf16[4,4,25,1024]{3,2,1,0:T(8,128)(2,1)} fusion(bf16[4,4,25,1024]{3,2,1,0:T(8,128)(2,1)} %get-tuple-element.1930, s32[]{:T(128)} %get-tuple-element.1928, f32[4,1,1024]{2,1,0:T(1,128)S(1)} %get-tuple-element.1514, f32[4,1,1024]{2,1,0:T(1,128)S(1)} %get-tuple-element.1530, ...), kind=kLoop, calls=%fused_computation.82.clone.1 | loop fusion | flops 7680000 | bytes 1491456 | tf_op jit(solution)/shard_map/while/body/jit(dynamic_update_index_in_dim)/dynamic_update_slice | solution.py:71
  162.1 3.4 %bitcast_dynamic-update-slice_fusion.4 = bf16[4,4,25,1024]{3,2,1,0:T(8,128)(2,1)} fusion(bf16[4,4,25,1024]{3,2,1,0:T(8,128)(2,1)} %get-tuple-element.1930, s32[]{:T(128)} %get-tuple-element.1928, f32[4,1,1024]{2,1,0:T(1,128)S(1)} %get-tuple-element.1514, f32[4,1,1024]{2,1,0:T(1,128)S(1)} %get-tuple-element.1530, ...), kind=kLoop, calls=%fused_computation.82.clone.1 | loop fusion | flops 7680000 | bytes 1491456 | tf_op jit(solution)/shard_map/while/body/jit(dynamic_update_index_in_dim)/dynamic_update_slice | solution.py:71
  170.4 4.6 %all-to-all-start.4 = ((bf16[32,25,1024]{2,1,0:T(8,128)(2,1)}), bf16[32,25,1024]{2,1,0:T(8,128)(2,1)}, u32[]{:S(2)}, u32[]{:S(2)}) async-start(bf16[32,25,1024]{2,1,0:T(8,128)(2,1)} %select_select_fusion.2), calls=%async_computation.4 | async-start | bytes 4194304 | tf_op jit(solution)/shard_map/all_to_all | solution.py:140
  175.0 31.0 %while.27 = (s32[]{:T(128)}, bf16[2,4,25,1024]{3,2,1,0:T(8,128)(2,1)S(1)}, s32[2,4,1024]{2,1,0:T(4,128)S(1)}, f32[2,4,1024]{2,1,0:T(4,128)S(1)}, bf16[2,4,8,1024...) while((s32[]{:T(128)}, bf16[2,4,25,1024]{3,2,1,0:T(8,128)(2,1)S(1)}, ...), condition=%wide.region_171.173_spmd, body=%wide.region_89.172_spmd.sunk | while | flops 22034952 | bytes 28743784 | solution.py:71
  187.7 2.8 %bitcast_dynamic-update-slice_fusion.5 = bf16[2,4,25,1024]{3,2,1,0:T(8,128)(2,1)S(1)} fusion(bf16[2,4,25,1024]{3,2,1,0:T(8,128)(2,1)S(1)} %get-tuple-element.1954, s32[]{:T(128)} %get-tuple-element.1953, f32[4,1,1024]{2,1,0:T(1,128)S(1)} %get-tuple-element.1784, f32[4,1,1024]{2,1,0:T(1,128)S(1)} %get-tuple-element.1800, ...), kind=kLoop, calls=%fused_computation.484.clone.1 | loop fusion | flops 7680000 | bytes 1490948 | tf_op jit(solution)/shard_map/while/body/jit(dynamic_update_index_in_dim)/dynamic_update_slice | solution.py:71
  203.2 2.8 %bitcast_dynamic-update-slice_fusion.5 = bf16[2,4,25,1024]{3,2,1,0:T(8,128)(2,1)S(1)} fusion(bf16[2,4,25,1024]{3,2,1,0:T(8,128)(2,1)S(1)} %get-tuple-element.1954, s32[]{:T(128)} %get-tuple-element.1953, f32[4,1,1024]{2,1,0:T(1,128)S(1)} %get-tuple-element.1784, f32[4,1,1024]{2,1,0:T(1,128)S(1)} %get-tuple-element.1800, ...), kind=kLoop, calls=%fused_computation.484.clone.1 | loop fusion | flops 7680000 | bytes 1490948 | tf_op jit(solution)/shard_map/while/body/jit(dynamic_update_index_in_dim)/dynamic_update_slice | solution.py:71
  207.6 15.1 %all-to-all-done.4 = bf16[32,25,1024]{2,1,0:T(8,128)(2,1)} async-done(((bf16[32,25,1024]{2,1,0:T(8,128)(2,1)}), bf16[32,25,1024]{2,1,0:T(8,128)(2,1)}, u32[]{:S(2)}, u32[]{:S(2)}) %all-to-all-start.4) | async-done | bytes 1638432 | tf_op jit(solution)/shard_map/all_to_all | solution.py:140
  222.7 2.3 gather_fusion.8
  225.3 2.1 copy.31
  (395 shorter events, 100.1 us)
Async XLA Ops:
  0.6 13.5 %copy-start = (bf16[1,1,32,8,1024]{4,3,2,1,0:T(8,128)(2,1)S(1)}, bf16[1,1,32,8,1024]{4,3,2,1,0:T(8,128)(2,1)}, u32[]{:S(2)}) copy-start(bf16[1,1,32,8,1024]{4,3,2,1,0:T(8,128)(2,1)} %param.17) | copy-start | bytes 1572868
  5.3 11.8 %all-to-all-start = ((bf16[4,8,1]{1,2,0:T(2,128)(2,1)}), bf16[4,8,1]{1,2,0:T(2,128)(2,1)S(1)}, u32[]{:S(2)}, u32[]{:S(2)}) async-start(bf16[4,8,1]{1,2,0:T(2,128)(2,1)} %copy.26), calls=%async_computation | async-start | bytes 4096 | tf_op jit(solution)/shard_map/all_to_all | solution.py:123
  17.1 9.0 %all-to-all-start.1 = ((bf16[4,8,1024]{2,1,0:T(8,128)(2,1)}), bf16[4,8,1024]{2,1,0:T(8,128)(2,1)S(1)}, u32[]{:S(2)}, u32[]{:S(2)}) async-start(bf16[4,8,1024]{2,1,0:T(8,128)(2,1)} %fusion.82), calls=%async_computation.1 | async-start | bytes 131072 | tf_op jit(solution)/shard_map/all_to_all | solution.py:122
  26.1 15.7 %all-to-all-start.2 = ((bf16[32,8,1024]{2,1,0:T(8,128)(2,1)}), bf16[32,8,1024]{2,1,0:T(8,128)(2,1)S(1)}, u32[]{:S(2)}, u32[]{:S(2)}) async-start(bf16[32,8,1024]{2,1,0:T(8,128)(2,1)} %select_select_fusion.3), calls=%async_computation.2 | async-start | bytes 1048576 | tf_op jit(solution)/shard_map/all_to_all | solution.py:121
  37.1 9.1 %copy-start.3 = (bf16[1,1,8,25,1024]{4,2,3,1,0:T(8,128)(2,1)S(1)}, bf16[1,1,8,25,1024]{4,2,3,1,0:T(8,128)(2,1)}, u32[]{:S(2)}) copy-start(bf16[1,1,8,25,1024]{4,2,3,1,0:T(8,128)(2,1)} %param.22) | copy-start | bytes 1228804
  37.1 9.4 %copy-start.4 = (s32[1,1,8,1024]{3,2,1,0:T(8,128)S(1)}, s32[1,1,8,1024]{3,2,1,0:T(8,128)}, u32[]{:S(2)}) copy-start(s32[1,1,8,1024]{3,2,1,0:T(8,128)} %param.25) | copy-start | bytes 98308
  37.2 9.4 %copy-start.5 = (s32[1,1,8,1024]{3,2,1,0:T(8,128)S(1)}, s32[1,1,8,1024]{3,2,1,0:T(8,128)}, u32[]{:S(2)}) copy-start(s32[1,1,8,1024]{3,2,1,0:T(8,128)} %param.24) | copy-start | bytes 98308
  41.8 49.5 %all-to-all-start.3 = ((bf16[32,25,1024]{2,1,0:T(8,128)(2,1)}), bf16[32,25,1024]{2,1,0:T(8,128)(2,1)}, u32[]{:S(2)}, u32[]{:S(2)}) async-start(bf16[32,25,1024]{2,1,0:T(8,128)(2,1)} %select_select_fusion.1), calls=%async_computation.3 | async-start | bytes 4194304 | tf_op jit(solution)/shard_map/all_to_all | solution.py:120
  166.8 1.9 copy-start.8
  166.8 1.9 copy-start.9
  170.4 4.6 %copy-start.1 = (bf16[1,1,8,8,1024]{4,3,2,1,0:T(8,128)(2,1)S(1)}, bf16[1,1,8,8,1024]{4,3,2,1,0:T(8,128)(2,1)}, u32[]{:S(2)}) copy-start(bf16[1,1,8,8,1024]{4,3,2,1,0:T(8,128)(2,1)} %param.23) | copy-start | bytes 393220
  170.4 4.6 %copy-start.2 = (bf16[2,4,25,1024]{3,2,1,0:T(8,128)(2,1)S(1)}, bf16[2,4,25,1024]{3,2,1,0:T(8,128)(2,1)}, u32[]{:S(2)}) copy-start(bf16[2,4,25,1024]{3,2,1,0:T(8,128)(2,1)} %custom-call.20) | copy-start | bytes 1228804
  170.4 52.3 %all-to-all-start.4 = ((bf16[32,25,1024]{2,1,0:T(8,128)(2,1)}), bf16[32,25,1024]{2,1,0:T(8,128)(2,1)}, u32[]{:S(2)}, u32[]{:S(2)}) async-start(bf16[32,25,1024]{2,1,0:T(8,128)(2,1)} %select_select_fusion.2), calls=%async_computation.4 | async-start | bytes 4194304 | tf_op jit(solution)/shard_map/all_to_all | solution.py:140
  175.0 32.0 %copy-start.7 = (s32[32]{0:T(128)S(1)}, s32[32]{0:T(128)}, u32[]{:S(2)}) copy-start(s32[32]{0:T(128)} %get-tuple-element.391) | copy-start | bytes 388
  175.0 32.0 %copy-start.6 = (f32[4,4]{1,0:T(4,128)S(1)}, f32[4,4]{1,0:T(4,128)}, u32[]{:S(2)}) copy-start(f32[4,4]{1,0:T(4,128)} %get-tuple-element.177) | copy-start | bytes 196
where the time goes:
time: 228 us; the launch traced here: 227 us
  other arithmetic  108 us (47%)
  waiting for transfers between devices  68.4 us (30%)
  local copies, waits for them, and re-layouts  25.5 us (11%)
  starting transfers between devices  22.1 us (10%)
    all_to_all x1, waiting for transfers between devices, on_device(): lax.all_to_all(send_taps, 'length', split_axis=0, concat_axis=0, tiled=True)  41.6 us
    reduce_sum x36, other arithmetic, message(): summed = summed + (tap_weights[tap_index] * inside)[None, :] * shifted  22.3 us
    dynamic_update_slice x6, other arithmetic, batched(): losses, slopes = lax.map(compute_block, shaped)  19.4 us
    reduce_sum x24, other arithmetic, normalize(): return raised / jnp.sum(raised, axis=0, keepdims=True)  15.2 us
    all_to_all x1, waiting for transfers between devices, on_device(): lax.all_to_all(sent_back, 'length', split_axis=0, concat_axis=0, tiled=True)  15.1 us
    mul x66, other arithmetic, message(): summed = summed + (tap_weights[tap_index] * inside)[None, :] * shifted  14.4 us
    add_any x12, other arithmetic, message(): lax.slice_in_dim(padded, margin + offset, margin + offset + pixels, axis=1)  9.06 us
    all_to_all x1, starting transfers between devices, on_device(): lax.all_to_all(note_slot.astype(jnp.bfloat16), 'length', split_axis=0, co...  6.32 us
  transfers between devices with their start and end apart: 5, of which 5 were waited for; matrix products, arithmetic and copies ran while one was open for 21% of the time, Pallas kernels for 0%

commit v1 on v0

v1 whole, which is shorter than its diff:
```python
import functools

import jax
import jax.numpy as jnp
from jax import lax
from jax.experimental import pallas as pl
from jax.experimental.pallas import tpu as pltpu
from jax.sharding import PartitionSpec as P

CLASSES = 8
DIFFS = CLASSES - 1
TAPS = 25
TILE = 32
ITERS = 3
RECV = 16
GROUP = 4
LANES = 128
PITCH = 40
TOP = 4
CHUNKS = 8
STEP = 4
F32 = jnp.float32


def unrolled(count, body):
    for index in range(count):
        body(index)


def looped(count, body):
    def step(index, carry):
        body(index)
        return carry

    lax.fori_loop(0, count, step, 0)


def swap_blocks(parts, lane):
    low_half = lane < 64
    even = (lane // TILE) % 2 == 0
    half = [None] * 4
    for j in (0, 1):
        half[j] = jnp.where(low_half, parts[j], pltpu.roll(parts[j + 2], 64, 1))
        half[j + 2] = jnp.where(low_half, pltpu.roll(parts[j], 64, 1), parts[j + 2])
    out = [None] * 4
    for j in (0, 2):
        out[j] = jnp.where(even, half[j], pltpu.roll(half[j + 1], TILE, 1))
        out[j + 1] = jnp.where(even, pltpu.roll(half[j], LANES - TILE, 1), half[j + 1])
    return out


def rows(base, phase):
    return pl.ds(base + phase, 8, stride=STEP)


def tile_kernel(flagged, ranks, *refs):
    if flagged:
        dest_ref, slot_ref, *refs = refs
    k_ref, u_ref, lab_ref, msk_ref, *refs = refs
    if flagged:
        out_ref, loss_ref, *refs = refs
    else:
        out_ref, *refs = refs
    kx, ux, lx, fields, beliefs, grads, acc, sums = refs
    group = pl.program_id(0)

    @pl.when(group == 0)
    def _():
        kx[...] = jnp.zeros_like(kx)
        fields[...] = jnp.zeros_like(fields)
        grads[...] = jnp.zeros_like(grads)
        if flagged:
            sums[...] = jnp.zeros_like(sums)

    def field_base(it, b, c):
        return ((it * 5 + b) * DIFFS + c) * PITCH + TOP

    def grad_base(it, c):
        return (it * DIFFS + c) * PITCH + TOP

    def work():
        lane25 = lax.broadcasted_iota(jnp.int32, (TAPS, LANES), 1)
        tap25 = lax.broadcasted_iota(jnp.int32, (TAPS, LANES), 0)
        seen = lane25 % TILE + tap25 % 5 - 2
        inside = ((seen >= 0) & (seen < TILE)).astype(F32)
        lane8 = lax.broadcasted_iota(jnp.int32, (8, LANES), 1)

        def bring(s):
            cut = pl.ds(s * LANES, LANES)
            parts = [k_ref[i, :, cut].astype(F32) for i in range(GROUP)]
            for r, value in enumerate(swap_blocks(parts, lane25)):
                kx[pl.ds(TOP + STEP * s + r, TAPS, stride=PITCH), :] = value * inside
            parts = [u_ref[i, :, cut].astype(F32) for i in range(GROUP)]
            for r, value in enumerate(swap_blocks(parts, lane8)):
                ux[pl.ds(STEP * s + r, CLASSES, stride=TILE), :] = value
            target = jnp.where(msk_ref[:, cut] == 1, lab_ref[:, cut], CLASSES)
            lx[pl.ds(s, 8, stride=8), :] = target

        unrolled(CHUNKS, bring)
        first = (group % 2) * GROUP
        labels = swap_blocks(
            [lx[pl.ds(pl.multiple_of(8 * (first + i), 8), 8), :] for i in range(GROUP)],
            lane8,
        )

        def spread(it, r, parts):
            for c, value in enumerate(parts):
                for b in range(5):
                    moved = value if b == 2 else pltpu.roll(value, (2 - b) % LANES, 1)
                    fields[rows(field_base(it, b, c), r), :] = moved

        def normalize(it, r, diffs):
            raised = [jnp.exp(d) for d in diffs]
            inverse = 1.0 / (functools.reduce(jnp.add, raised) + 1.0)
            spread(it, r, [(e - 1.0) * inverse for e in raised])
            if it > 0:
                for c in range(DIFFS):
                    beliefs[pl.ds(((it - 1) * DIFFS + c) * TILE + 8 * r, 8), :] = (
                        raised[c] * inverse
                    )

        for r in range(STEP):
            last = ux[pl.ds((CLASSES - 1) * TILE + r, 8, stride=STEP), :]
            diffs = [
                ux[pl.ds(c * TILE + r, 8, stride=STEP), :] - last for c in range(DIFFS)
            ]
            for c in range(DIFFS):
                ux[pl.ds(c * TILE + r, 8, stride=STEP), :] = diffs[c]
            normalize(0, r, diffs)

        for it in range(ITERS):
            for b in range(5):
                taps = [
                    [kx[rows((5 * a + b) * PITCH + TOP, r), :] for r in range(STEP)]
                    for a in range(5)
                ]
                for c in range(DIFFS):
                    near = [
                        fields[rows(field_base(it, b, c), r - 2), :] for r in range(8)
                    ]
                    for r in range(STEP):
                        place = pl.ds((c * STEP + r) * 8, 8)
                        if b == 0:
                            total = ux[pl.ds(c * TILE + r, 8, stride=STEP), :]
                        else:
                            total = acc[place, :]
                        for a in range(5):
                            total = total + taps[a][r] * near[r + a]
                        acc[place, :] = total
            if it + 1 < ITERS:
                for r in range(STEP):
                    normalize(
                        it + 1,
                        r,
                        [acc[pl.ds((c * STEP + r) * 8, 8), :] for c in range(DIFFS)],
                    )

        lost = jnp.zeros((8, LANES), F32)
        for r in range(STEP):
            diffs = [acc[pl.ds((c * STEP + r) * 8, 8), :] for c in range(DIFFS)]
            raised = [jnp.exp(d) for d in diffs]
            total = functools.reduce(jnp.add, raised) + 1.0
            inverse = 1.0 / total
            counted = labels[r] < CLASSES
            chosen = jnp.zeros((8, LANES), F32)
            for c in range(DIFFS):
                hit = labels[r] == c
                chosen = jnp.where(hit, diffs[c], chosen)
                slope = raised[c] * inverse - hit.astype(F32)
                grads[rows(grad_base(ITERS - 1, c), r), :] = jnp.where(
                    counted, slope, 0.0
                )
            lost = lost + jnp.where(counted, jnp.log(total) - chosen, 0.0)
        if flagged:
            sums[pl.ds(group, 1), :] = jnp.sum(lost, axis=0, keepdims=True)

        for it in range(ITERS - 1, 0, -1):
            for b in range(5):
                taps = [
                    [
                        kx[rows((5 * a + b) * PITCH + TOP, r - (a - 2)), :]
                        for r in range(STEP)
                    ]
                    for a in range(5)
                ]
                for c in range(DIFFS):
                    near = [
                        grads[rows(grad_base(it, c), r - 2), :] for r in range(8)
                    ]
                    for r in range(STEP):
                        place = pl.ds((c * STEP + r) * 8, 8)
                        total = taps[0][r] * near[r + 4]
                        for a in range(1, 5):
                            total = total + taps[a][r] * near[r + 4 - a]
                        if b != 2:
                            total = pltpu.roll(total, (b - 2) % LANES, 1)
                        if b > 0:
                            total = total + acc[place, :]
                        acc[place, :] = total
            for r in range(STEP):
                back = [acc[pl.ds((c * STEP + r) * 8, 8), :] for c in range(DIFFS)]
                mean = functools.reduce(
                    jnp.add,
                    [
                        back[c] * fields[rows(field_base(it, 2, c), r), :]
                        for c in range(DIFFS)
                    ],
                )
                for c in range(DIFFS):
                    belief = beliefs[pl.ds(((it - 1) * DIFFS + c) * TILE + 8 * r, 8), :]
                    grads[rows(grad_base(it - 1, c), r), :] = belief * (back[c] - mean)

        for b in range(5):
            totals = [[None] * STEP for _ in range(5)]
            for it in range(ITERS):
                for c in range(DIFFS):
                    near = [
                        fields[rows(field_base(it, b, c), r - 2), :] for r in range(8)
                    ]
                    for r in range(STEP):
                        slope = grads[rows(grad_base(it, c), r), :]
                        for a in range(5):
                            term = slope * near[r + a]
                            old = totals[a][r]
                            totals[a][r] = term if old is None else old + term
            for a in range(5):
                for r in range(STEP):
                    kx[rows((5 * a + b) * PITCH + TOP, r), :] = totals[a][r]

        def give(s):
            cut = pl.ds(s * LANES, LANES)
            parts = [
                kx[pl.ds(TOP + STEP * s + r, TAPS, stride=PITCH), :] * inside
                for r in range(STEP)
            ]
            for i, value in enumerate(swap_blocks(parts, lane25)):
                if flagged:
                    live = dest_ref[group * GROUP + i] >= 0
                    value = jnp.where(live, value, 0.0)
                out_ref[i, :, cut] = value.astype(jnp.bfloat16)

        unrolled(CHUNKS, give)

    if not flagged:
        work()
        return

    @pl.when(dest_ref[group * GROUP] >= 0)
    def _():
        work()

    @pl.when(dest_ref[group * GROUP] < 0)
    def _():
        out_ref[...] = jnp.zeros_like(out_ref)

    @pl.when(group == pl.num_programs(0) - 1)
    def _():
        lane = lax.broadcasted_iota(jnp.int32, sums.shape, 1)
        for i in range(GROUP):
            one = jnp.where(lane // TILE == i, sums[...], 0.0)
            one = jnp.sum(one, axis=1, keepdims=True) * (1.0 / TILE)
            acc[pl.ds(i * sums.shape[0], sums.shape[0]), :] = jnp.broadcast_to(
                one, sums.shape
            )
        spot = lax.broadcasted_iota(
            jnp.int32, (ranks, LANES), 0
        ) * LANES + lax.broadcasted_iota(jnp.int32, (ranks, LANES), 1)
        placed = jnp.zeros((ranks, LANES), F32)
        for j in range(sums.shape[0] * GROUP):
            here = dest_ref[j] * LANES + slot_ref[j]
            row = (j % GROUP) * sums.shape[0] + j // GROUP
            value = acc[pl.ds(row, 1), :]
            placed = jnp.where(spot == here, value, placed)
        loss_ref[...] = placed


def process(kernels, unary, labels, mask, lists, ranks):
    count = kernels.shape[0]
    steps = count // GROUP
    flagged = lists is not None

    def whole(*shape):
        return pl.BlockSpec(shape, lambda g, *_: (0,) * len(shape))

    def part(*shape):
        return pl.BlockSpec(shape, lambda g, *_: (g,) + (0,) * (len(shape) - 1))

    pixels = TILE * TILE
    out_shape = [jax.ShapeDtypeStruct(kernels.shape, jnp.bfloat16)]
    out_specs = [part(GROUP, TAPS, pixels)]
    if flagged:
        out_shape.append(jax.ShapeDtypeStruct((ranks, LANES), F32))
        out_specs.append(whole(ranks, LANES))
    return pl.pallas_call(
        functools.partial(tile_kernel, flagged, ranks),
        out_shape=out_shape,
        grid_spec=pltpu.PrefetchScalarGridSpec(
            num_scalar_prefetch=2 if flagged else 0,
            grid=(steps,),
            in_specs=[
                part(GROUP, TAPS, pixels),
                part(GROUP, CLASSES, pixels),
                pl.BlockSpec((8, pixels), lambda g, *_: (g // 2, 0)),
                pl.BlockSpec((8, pixels), lambda g, *_: (g // 2, 0)),
            ],
            out_specs=out_specs,
            scratch_shapes=[
                pltpu.VMEM((TAPS * PITCH, LANES), F32),
                pltpu.VMEM((CLASSES * TILE, LANES), F32),
                pltpu.VMEM((8 * 8, LANES), jnp.int32),
                pltpu.VMEM((ITERS * 5 * DIFFS * PITCH, LANES), F32),
                pltpu.VMEM(((ITERS - 1) * DIFFS * TILE, LANES), F32),
                pltpu.VMEM((ITERS * DIFFS * PITCH, LANES), F32),
                pltpu.VMEM((DIFFS * TILE, LANES), F32),
                pltpu.VMEM((max(8, steps), LANES), F32),
            ],
        ),
        compiler_params=pltpu.CompilerParams(vmem_limit_bytes=32 * 1024 * 1024),
        name="flag_tiles" if flagged else "res_tiles",
    )(*(lists if flagged else ()), kernels, unary, labels, mask)


def on_device(
    flag_kernels,
    flag_unary,
    flag_labels,
    flag_mask,
    dest_list,
    slot_list,
    res_kernels,
    res_unary,
    res_labels,
    res_mask,
):
    ranks = lax.axis_size("length")
    flag_grad, placed = process(
        flag_kernels[0, 0],
        flag_unary[0, 0],
        flag_labels[0, 0],
        flag_mask[0, 0],
        (dest_list[0, 0], slot_list[0, 0]),
        ranks,
    )
    got = lax.all_to_all(placed, "length", split_axis=0, concat_axis=0, tiled=True)
    (res_grad,) = process(
        res_kernels[0, 0], res_unary[0, 0], res_labels[0, 0], res_mask[0, 0], None, ranks
    )
    helper_loss = jnp.sum(got, axis=0)[:RECV]
    return flag_grad[None, None], res_grad[None, None], helper_loss[None, None]


def solution(mesh):
    tiles = ("groups", "sector", "pair")
    spec = lambda extra: P("length", tiles, *([None] * extra))
    in_specs = tuple(spec(n) for n in (3, 3, 2, 2, 1, 1, 3, 3, 2, 2))
    out_specs = tuple(spec(n) for n in (3, 3, 1))
    return jax.shard_map(
        on_device, mesh=mesh, in_specs=in_specs, out_specs=out_specs, check_vma=False
    )
```

time: 228 us -> 53 us (0.23)
  the two profiles are of different devices: /device:TPU:0 before, /device:TPU:11 now
where the time goes in v1:
time: 53 us; the launch traced here: 52.8 us
  starting transfers between devices  23.9 us (45%)
  Pallas kernels  21.8 us (41%)
  local copies, waits for them, and re-layouts  6.32 us (12%)
  between operations  0.76 us (1%)
    all_to_all x1, starting transfers between devices, on_device(): lax.all_to_all(placed, 'length', split_axis=0, concat_axis=0, tiled=True)  23.9 us
    pallas_call x2, Pallas kernels, process(): pl.pallas_call(functools.partial(tile_kernel, flagged, ranks), out_shape=...  21.8 us
    unnamed x22, local copies, waits for them, and re-layouts  5.8 us
  transfers between devices with their start and end apart: 1, of which 0 were waited for; matrix products, arithmetic and copies ran while one was open for 6% of the time, Pallas kernels for 16%

profile of v1, /device:TPU:11, one launch (start us, length us, event | category | flops | bytes accessed | tf_op | source)
XLA Modules:
  0.0 52.8 jit_solution(13994316645337766778)
XLA Ops:
  0.6 0.0 copy-start.6
  0.6 0.0 copy-start.7
  0.7 0.0 copy-start
  0.7 0.0 copy-start.2
  0.7 0.0 copy-start.3
  0.7 2.4 %copy.24 = bf16[1,1,32,25,1024]{4,3,2,1,0:T(8,128)(2,1)S(1)} copy(bf16[1,1,32,25,1024]{4,2,3,1,0:T(8,128)(2,1)} %param.10) | data formatting | bytes 3276800 | tf_op args[0]
  3.1 0.0 copy-done.6
  3.1 0.0 copy-done.7
  3.2 0.0 copy-done
  3.2 0.0 copy-done.2
  3.2 0.0 copy-done.3
  3.2 13.4 %flag_tiles.1 = (bf16[32,25,1024]{2,1,0:T(8,128)(2,1)S(1)}, f32[4,128]{1,0:T(4,128)}) custom-call(s32[32]{0:T(128)S(1)} %bitcast.31, s32[32]{0:T(128)S(1)} %bitcast.32, bf16[32,25,1024]{2,1,0:T(8,128)(2,1)S(1)} %bitcast.21, bf16[32,8,1024]{2,1,0:T(8,128)(2,1)S(1)} %bitcast.25, s32[32,1024]{1,0:T(8,128)S(1)} %bitcast.27, s32[32,1024]{1,0:T(8,128)S(1)} %bitcast.28), custom_call_target="tpu_custom_call" | custom-call | tf_op jit(solution)/shard_map/flag_tiles/pallas_call | solution.py:294
  16.6 0.0 copy-start.8
  16.6 23.9 %all-to-all-start = ((f32[4,1,128]{2,1,0:T(1,128)}), f32[4,1,128]{2,1,0:T(1,128)S(1)}, u32[]{:S(2)}, u32[]{:S(2)}) async-start(f32[4,1,128]{2,1,0:T(1,128)} %bitcast.13), calls=%async_computation | async-start | bytes 4096 | tf_op jit(solution)/shard_map/all_to_all | solution.py:344
  40.5 2.1 %copy.20 = bf16[1,1,32,25,1024]{4,2,3,1,0:T(8,128)(2,1)} copy(bf16[1,1,32,25,1024]{4,3,2,1,0:T(8,128)(2,1)S(1)} %bitcast.22) | data formatting | bytes 3276800
  42.6 0.0 copy-done.8
  42.6 0.2 copy.25
  42.8 0.0 copy-done.1
  42.8 0.0 copy-done.4
  42.8 0.0 copy-done.5
  42.8 8.5 %res_tiles.1 = bf16[8,25,1024]{2,1,0:T(8,128)(2,1)S(1)} custom-call(bf16[8,25,1024]{2,1,0:T(8,128)(2,1)S(1)} %bitcast.24, bf16[8,8,1024]{2,1,0:T(8,128)(2,1)S(1)} %bitcast.26, s32[8,1024]{1,0:T(8,128)S(1)} %bitcast.29, s32[8,1024]{1,0:T(8,128)S(1)} %bitcast.30), custom_call_target="tpu_custom_call" | custom-call | tf_op jit(solution)/shard_map/res_tiles/pallas_call | solution.py:294
  51.3 1.0 %copy.21 = bf16[1,1,8,25,1024]{4,2,3,1,0:T(8,128)(2,1)} copy(bf16[1,1,8,25,1024]{4,3,2,1,0:T(8,128)(2,1)S(1)} %bitcast.23) | data formatting | bytes 819200
  52.3 0.0 all-to-all-done
  52.3 0.5 slice_bitcast_fusion
  (4 shorter events, 0.0 us)
Async XLA Ops:
  0.6 2.5 %copy-start.6 = (s32[1,1,32]{2,1,0:T(1,128)S(1)}, s32[1,1,32]{2,1,0:T(1,128)}, u32[]{:S(2)}) copy-start(s32[1,1,32]{2,1,0:T(1,128)} %param.14) | copy-start | bytes 388
  0.6 2.5 %copy-start.7 = (s32[1,1,32]{2,1,0:T(1,128)S(1)}, s32[1,1,32]{2,1,0:T(1,128)}, u32[]{:S(2)}) copy-start(s32[1,1,32]{2,1,0:T(1,128)} %param.15) | copy-start | bytes 388
  0.7 2.5 %copy-start = (bf16[1,1,32,8,1024]{4,3,2,1,0:T(8,128)(2,1)S(1)}, bf16[1,1,32,8,1024]{4,3,2,1,0:T(8,128)(2,1)}, u32[]{:S(2)}) copy-start(bf16[1,1,32,8,1024]{4,3,2,1,0:T(8,128)(2,1)} %param.11) | copy-start | bytes 1572868
  0.7 2.5 %copy-start.2 = (s32[1,1,32,1024]{3,2,1,0:T(8,128)S(1)}, s32[1,1,32,1024]{3,2,1,0:T(8,128)}, u32[]{:S(2)}) copy-start(s32[1,1,32,1024]{3,2,1,0:T(8,128)} %param.12) | copy-start | bytes 393220
  0.7 2.5 %copy-start.3 = (s32[1,1,32,1024]{3,2,1,0:T(8,128)S(1)}, s32[1,1,32,1024]{3,2,1,0:T(8,128)}, u32[]{:S(2)}) copy-start(s32[1,1,32,1024]{3,2,1,0:T(8,128)} %param.13) | copy-start | bytes 393220
  16.6 26.0 %copy-start.8 = (bf16[1,1,8,25,1024]{4,2,3,1,0:T(8,128)(2,1)S(1)}, bf16[1,1,8,25,1024]{4,2,3,1,0:T(8,128)(2,1)}, u32[]{:S(2)}) copy-start(bf16[1,1,8,25,1024]{4,2,3,1,0:T(8,128)(2,1)} %param.16) | copy-start | bytes 1228804
  16.6 35.7 %all-to-all-start = ((f32[4,1,128]{2,1,0:T(1,128)}), f32[4,1,128]{2,1,0:T(1,128)S(1)}, u32[]{:S(2)}, u32[]{:S(2)}) async-start(f32[4,1,128]{2,1,0:T(1,128)} %bitcast.13), calls=%async_computation | async-start | bytes 4096 | tf_op jit(solution)/shard_map/all_to_all | solution.py:344
  40.4 2.4 %copy-start.1 = (bf16[1,1,8,8,1024]{4,3,2,1,0:T(8,128)(2,1)S(1)}, bf16[1,1,8,8,1024]{4,3,2,1,0:T(8,128)(2,1)}, u32[]{:S(2)}) copy-start(bf16[1,1,8,8,1024]{4,3,2,1,0:T(8,128)(2,1)} %param.17) | copy-start | bytes 393220
  40.4 2.4 %copy-start.4 = (s32[1,1,8,1024]{3,2,1,0:T(8,128)S(1)}, s32[1,1,8,1024]{3,2,1,0:T(8,128)}, u32[]{:S(2)}) copy-start(s32[1,1,8,1024]{3,2,1,0:T(8,128)} %param.18) | copy-start | bytes 98308
  40.4 2.4 %copy-start.5 = (s32[1,1,8,1024]{3,2,1,0:T(8,128)S(1)}, s32[1,1,8,1024]{3,2,1,0:T(8,128)}, u32[]{:S(2)}) copy-start(s32[1,1,8,1024]{3,2,1,0:T(8,128)} %param.19) | copy-start | bytes 98308

commit v2 on v0

v2 whole, which is shorter than its diff:
```python
import functools

import jax
import jax.numpy as jnp
from jax import lax
from jax.experimental import pallas as pl
from jax.experimental.pallas import tpu as pltpu
from jax.sharding import PartitionSpec as P

CLASSES = 8
DIFFS = CLASSES - 1
TAPS = 25
TILE = 32
ITERS = 3
RECV = 16
LANES = 128
BLOCKS = 4
ROWS = 8
PIXELS = TILE * TILE
FIELD = ROWS * DIFFS * 8
PAIR = FIELD // 4
HALOED = 6 * PAIR
SPREAD = 5 * HALOED
SCORES = (CLASSES + 2) * 8
F32 = jnp.float32
BF16 = jnp.bfloat16


def dot(left, right):
    return jnp.dot(left, right, preferred_element_type=F32)


def tile_kernel(flagged, width, ranks, *refs):
    if flagged:
        dest_ref, slot_ref, me_ref, *refs = refs
    k_ref, u_ref, lab_ref, msk_ref, out_ref, *refs = refs
    if flagged:
        loss_refs, refs = refs[:ranks], refs[ranks:]
    swap, move, down, up, kx, kt, uu, ux, ud, acc, hl, fields, beliefs, grads, sums = refs
    block = pl.program_id(0)
    halves = width // 8

    @pl.when(block == 0)
    def _():
        row = lax.broadcasted_iota(jnp.int32, (LANES, LANES), 0)
        lane = lax.broadcasted_iota(jnp.int32, (LANES, LANES), 1)
        same = row % TILE == lane % TILE
        for j in range(BLOCKS):
            for r in range(BLOCKS):
                hit = same & (row // TILE == r) & (lane // TILE == j)
                swap[pl.ds(j * LANES, LANES), pl.ds(r * LANES, LANES)] = jnp.where(
                    hit, 1.0, 0.0
                ).astype(BF16)
        for b in range(5):
            seen = lane % TILE + b - 2
            inside = (seen >= 0) & (seen < TILE)
            for ref, jump in ((move, 0), (down, -TILE), (up, TILE)):
                place = b
                if jump == 0:
                    if b == 2:
                        continue
                    place = b - (b > 2)
                hit = inside & (row == lane + b - 2 + jump)
                part = jnp.where(hit, 1.0, 0.0).astype(BF16)
                for twice in range(2):
                    ref[pl.ds(twice * LANES, LANES), pl.ds(place * LANES, LANES)] = part
        uu[...] = jnp.zeros_like(uu)
        if flagged:
            sums[...] = jnp.zeros_like(sums)

    if flagged:
        live = jnp.int32(0)
        for j in range(sums.shape[0]):
            live = live + (dest_ref[j] >= 0).astype(jnp.int32)
    else:
        live = jnp.int32(width)
    active = jnp.clip((live - block * width + 7) // 8, 0, halves)

    def kernel_at(t, r):
        return ((r % 4) * 2 + r // 4) * TAPS + t

    def field_at(slot, b, r, c):
        return slot * SPREAD + ((b * 6 + (r + 2) // 2) * DIFFS + c) * 16 + (r % 2) * 8

    def plain_at(r, c):
        return ((r // 2) * DIFFS + c) * 16 + (r % 2) * 8

    def eight(start):
        return pl.ds(pl.multiple_of(start, 8), 8)

    def sixteen(start):
        return pl.ds(pl.multiple_of(start, 16), 16)

    def bring_kernels():
        for p in range(2):
            parts = []
            for j in range(BLOCKS):
                part = k_ref[:, :, pl.ds((2 * j + p) * LANES, LANES)]
                if width % 16:
                    part = part.astype(F32).reshape(TAPS * width, LANES).astype(BF16)
                else:
                    part = part.reshape(TAPS * width, LANES)
                parts.append(part)
            left = jnp.concatenate(parts, axis=1)
            for r in range(BLOCKS):
                got = dot(left, swap[:, pl.ds(r * LANES, LANES)])
                kx[pl.ds((r * 2 + p) * TAPS, TAPS), :, :] = got.reshape(
                    TAPS, width, LANES
                )

    def give_kernels():
        for p in range(2):
            left = jnp.concatenate(
                [
                    kx[pl.ds((r * 2 + p) * TAPS, TAPS), :, :]
                    .reshape(TAPS * width, LANES)
                    .astype(BF16)
                    for r in range(BLOCKS)
                ],
                axis=1,
            )
            for j in range(BLOCKS):
                got = dot(left, swap[:, pl.ds(j * LANES, LANES)])
                out_ref[:, :, pl.ds((2 * j + p) * LANES, LANES)] = got.reshape(
                    TAPS, width, LANES
                ).astype(BF16)

    def emit(slot, pair, c, value):
        fields[sixteen(field_at(slot, 2, 2 * pair, c)), :] = value
        high = value.astype(BF16)
        low = (value - high.astype(F32)).astype(BF16)
        place = pl.ds((pair * DIFFS + c) * 16, 16)
        hl[place, pl.ds(0, LANES)] = high
        hl[place, pl.ds(LANES, LANES)] = low

    def shift(slot):
        base = slot * SPREAD

        def put(b, pair, count, value):
            start = pl.multiple_of(base + (b * 6 + pair) * PAIR, 16)
            fields[pl.ds(start, count * PAIR), :] = value

        for n, b in enumerate((0, 1, 3, 4)):
            put(b, 1, 4, dot(hl[...], move[:, pl.ds(n * LANES, LANES)]))
        for b in range(5):
            cut = pl.ds(b * LANES, LANES)
            put(b, 0, 1, dot(hl[pl.ds(3 * PAIR, PAIR), :], down[:, cut]))
            put(b, 5, 1, dot(hl[pl.ds(0, PAIR), :], up[:, cut]))

    def message(taps_ref, mine, slot, start_ref):
        for b in range(5):
            for half in range(2):
                taps = [
                    [taps_ref[kernel_at(5 * a + b, 4 * half + r), mine, :] for r in range(4)]
                    for a in range(5)
                ]
                for c in range(DIFFS):
                    near = [
                        fields[eight(field_at(slot, b, 4 * half + r - 2, c)), :]
                        for r in range(8)
                    ]
                    for r in range(4):
                        place = pl.ds(plain_at(4 * half + r, c), 8)
                        if b == 0:
                            total = None if start_ref is None else start_ref[place, :]
                        else:
                            total = acc[place, :]
                        for a in range(5):
                            term = taps[a][r] * near[r + a]
                            total = term if total is None else total + term
                        acc[place, :] = total

    def work(h, carry):
        mine = pl.ds(pl.multiple_of(8 * h, 8), 8)

        for a in range(5):
            for b in range(5):
                for r in range(ROWS):
                    source = r - (a - 2)
                    turn = b - 2
                    if source < 0:
                        source, turn = source + ROWS, turn + TILE
                    elif source >= ROWS:
                        source, turn = source - ROWS, turn - TILE
                    value = kx[kernel_at(5 * a + b, source), mine, :]
                    if turn:
                        value = pltpu.roll(value, turn % LANES, 1)
                    kt[kernel_at(5 * (4 - a) + 4 - b, r), mine, :] = value

        index = block * width + 8 * h
        counted = lax.broadcasted_iota(jnp.int32, (8, LANES), 0) + index < live
        for s in range(8):
            cut = pl.ds(s * LANES, LANES)
            for i in range(8):
                uu[pl.ds(s * SCORES + i, CLASSES, stride=8), :] = u_ref[
                    8 * h + i, :, cut
                ].astype(F32)
            target = jnp.where(
                counted & (msk_ref[mine, cut] == 1), lab_ref[mine, cut], CLASSES
            )
            uu[pl.ds(s * SCORES + 8 * CLASSES, 8), :] = target.astype(F32)
        left = jnp.concatenate(
            [
                jnp.concatenate(
                    [
                        uu[pl.ds((2 * j + p) * SCORES, SCORES), :].astype(BF16)
                        for j in range(BLOCKS)
                    ],
                    axis=1,
                )
                for p in range(2)
            ],
            axis=0,
        )
        for r in range(BLOCKS):
            ux[pl.ds(r * 2 * SCORES, 2 * SCORES), :] = dot(
                left, swap[:, pl.ds(r * LANES, LANES)]
            )

        def score(r, f):
            return ux[pl.ds((r % 4) * 2 * SCORES + (r // 4) * SCORES + 8 * f, 8), :]

        for r in range(ROWS):
            last = score(r, CLASSES - 1)
            for c in range(DIFFS):
                value = score(r, c) - last
                ud[pl.ds(plain_at(r, c), 8), :] = value
                acc[pl.ds(plain_at(r, c), 8), :] = value

        def forward(it, carry):
            for pair in range(4):
                at = lambda c: pl.ds((pair * DIFFS + c) * 16, 16)
                raised = [jnp.exp(acc[at(c), :]) for c in range(DIFFS)]
                inverse = 1.0 / (functools.reduce(jnp.add, raised) + 1.0)
                for c in range(DIFFS):
                    belief = raised[c] * inverse
                    beliefs[sixteen(it * FIELD + (pair * DIFFS + c) * 16), :] = belief
                    emit(it, pair, c, belief - inverse)
            shift(it)
            message(kx, mine, it, ud)
            return carry

        lax.fori_loop(0, ITERS, forward, 0)

        lost = jnp.zeros((8, LANES), F32)
        for r in range(ROWS):
            label = score(r, CLASSES)
            diffs = [acc[pl.ds(plain_at(r, c), 8), :] for c in range(DIFFS)]
            raised = [jnp.exp(d) for d in diffs]
            total = functools.reduce(jnp.add, raised) + 1.0
            inverse = 1.0 / total
            used = label < CLASSES
            chosen = jnp.zeros((8, LANES), F32)
            for c in range(DIFFS):
                hit = label == c
                chosen = jnp.where(hit, diffs[c], chosen)
                slope = raised[c] * inverse - jnp.where(hit, 1.0, 0.0)
                grads[pl.ds((ITERS - 1) * FIELD + plain_at(r, c), 8), :] = jnp.where(
                    used, slope, 0.0
                )
            lost = lost + jnp.where(used, jnp.log(total) - chosen, 0.0)
        if flagged:
            lost = jnp.sum(lost, axis=1, keepdims=True) * (1.0 / TILE)
            sums[eight(index), :] = jnp.broadcast_to(lost, (8, LANES))

        def backward(step, carry):
            it = ITERS - 1 - step
            for pair in range(4):
                for c in range(DIFFS):
                    place = (pair * DIFFS + c) * 16
                    emit(ITERS, pair, c, grads[sixteen(it * FIELD + place), :])
            shift(ITERS)
            message(kt, mine, ITERS, None)
            for pair in range(4):
                at = lambda c: (pair * DIFFS + c) * 16
                back = [acc[pl.ds(at(c), 16), :] for c in range(DIFFS)]
                mean = functools.reduce(
                    jnp.add,
                    [
                        back[c] * fields[sixteen(field_at(it, 2, 2 * pair, c)), :]
                        for c in range(DIFFS)
                    ],
                )
                for c in range(DIFFS):
                    belief = beliefs[sixteen(it * FIELD + at(c)), :]
                    grads[sixteen((it - 1) * FIELD + at(c)), :] = belief * (back[c] - mean)
            return carry

        lax.fori_loop(0, ITERS - 1, backward, 0)

        for b in range(5):
            for half in range(2):
                totals = [[None] * 4 for _ in range(5)]
                for it in range(ITERS):
                    for c in range(DIFFS):
                        near = [
                            fields[pl.ds(field_at(it, b, 4 * half + r - 2, c), 8), :]
                            for r in range(8)
                        ]
                        for r in range(4):
                            slope = grads[
                                pl.ds(it * FIELD + plain_at(4 * half + r, c), 8), :
                            ]
                            for a in range(5):
                                term = slope * near[r + a]
                                old = totals[a][r]
                                totals[a][r] = term if old is None else old + term
                for a in range(5):
                    for r in range(4):
                        kx[kernel_at(5 * a + b, 4 * half + r), mine, :] = totals[a][r]
        return carry

    def zero(h, carry):
        mine = pl.ds(pl.multiple_of(8 * h, 8), 8)
        kx[:, mine, :] = jnp.zeros((kx.shape[0], 8, LANES), F32)
        return carry

    @pl.when(active > 0)
    def _():
        bring_kernels()
        lax.fori_loop(0, active, work, 0)
        if flagged:
            lax.fori_loop(active, halves, zero, 0)
        give_kernels()

    if not flagged:
        return

    @pl.when(active == 0)
    def _():
        out_ref[...] = jnp.zeros_like(out_ref)

    @pl.when(block == pl.num_programs(0) - 1)
    def _():
        high = -(-ranks // 8) * 8
        spot = lax.broadcasted_iota(
            jnp.int32, (high, LANES), 0
        ) * LANES + lax.broadcasted_iota(jnp.int32, (high, LANES), 1)
        placed = jnp.zeros((high, LANES), F32)
        for j in range(sums.shape[0]):
            far = dest_ref[j] - me_ref[0]
            far = jnp.where(far < 0, far + ranks, far)
            here = jnp.where(dest_ref[j] >= 0, far * LANES + slot_ref[j], -1)
            placed = jnp.where(spot == here, sums[pl.ds(j, 1), :], placed)
        for k, ref in enumerate(loss_refs):
            ref[...] = placed[k : k + 1, :]


def process(kernels, unary, labels, mask, lists, ranks):
    kernels = jnp.transpose(kernels, (1, 0, 2))
    count = kernels.shape[1]
    flagged = lists is not None
    width = 16 if count % 16 == 0 else 8

    out_shape = [jax.ShapeDtypeStruct(kernels.shape, BF16)]
    out_specs = [pl.BlockSpec((TAPS, width, PIXELS), lambda g, *_: (0, g, 0))]
    if flagged:
        out_shape += [jax.ShapeDtypeStruct((1, LANES), F32)] * ranks
        out_specs += [pl.BlockSpec((1, LANES), lambda g, *_: (0, 0))] * ranks
    grads, *rows = pl.pallas_call(
        functools.partial(tile_kernel, flagged, width, ranks),
        out_shape=out_shape,
        grid_spec=pltpu.PrefetchScalarGridSpec(
            num_scalar_prefetch=3 if flagged else 0,
            grid=(count // width,),
            in_specs=[
                pl.BlockSpec((TAPS, width, PIXELS), lambda g, *_: (0, g, 0)),
                pl.BlockSpec((width, CLASSES, PIXELS), lambda g, *_: (g, 0, 0)),
                pl.BlockSpec((width, PIXELS), lambda g, *_: (g, 0)),
                pl.BlockSpec((width, PIXELS), lambda g, *_: (g, 0)),
            ],
            out_specs=out_specs,
            scratch_shapes=[
                pltpu.VMEM((BLOCKS * LANES, BLOCKS * LANES), BF16),
                pltpu.VMEM((2 * LANES, 4 * LANES), BF16),
                pltpu.VMEM((2 * LANES, 5 * LANES), BF16),
                pltpu.VMEM((2 * LANES, 5 * LANES), BF16),
                pltpu.VMEM((ROWS * TAPS, width, LANES), F32),
                pltpu.VMEM((ROWS * TAPS, width, LANES), F32),
                pltpu.VMEM((8 * SCORES, LANES), F32),
                pltpu.VMEM((8 * SCORES, LANES), F32),
                pltpu.VMEM((FIELD, LANES), F32),
                pltpu.VMEM((FIELD, LANES), F32),
                pltpu.VMEM((FIELD, 2 * LANES), BF16),
                pltpu.VMEM(((ITERS + 1) * SPREAD, LANES), F32),
                pltpu.VMEM((ITERS * FIELD, LANES), F32),
                pltpu.VMEM((ITERS * FIELD, LANES), F32),
                pltpu.VMEM((count, LANES), F32),
            ],
        ),
        compiler_params=pltpu.CompilerParams(vmem_limit_bytes=40 * 1024 * 1024),
        name="flag_tiles" if flagged else "res_tiles",
    )(*(lists if flagged else ()), kernels, unary, labels, mask)
    return jnp.transpose(grads, (1, 0, 2)), rows


def on_device(
    flag_kernels,
    flag_unary,
    flag_labels,
    flag_mask,
    dest_list,
    slot_list,
    res_kernels,
    res_unary,
    res_labels,
    res_mask,
):
    ranks = lax.axis_size("length")
    me = lax.axis_index("length").astype(jnp.int32).reshape(1)
    flag_grad, rows = process(
        flag_kernels[0, 0],
        flag_unary[0, 0],
        flag_labels[0, 0],
        flag_mask[0, 0],
        (dest_list[0, 0], slot_list[0, 0], me),
        ranks,
    )
    got = [rows[0]] + [
        lax.ppermute(rows[k], "length", [(i, (i + k) % ranks) for i in range(ranks)])
        for k in range(1, ranks)
    ]
    res_grad, _ = process(
        res_kernels[0, 0], res_unary[0, 0], res_labels[0, 0], res_mask[0, 0], None, ranks
    )
    helper_loss = functools.reduce(jnp.add, got)[:, :RECV]
    return flag_grad[None, None], res_grad[None, None], helper_loss[None]


def solution(mesh):
    tiles = ("groups", "sector", "pair")
    spec = lambda extra: P("length", tiles, *([None] * extra))
    in_specs = tuple(spec(n) for n in (3, 3, 2, 2, 1, 1, 3, 3, 2, 2))
    out_specs = tuple(spec(n) for n in (3, 3, 1))
    return jax.shard_map(
        on_device, mesh=mesh, in_specs=in_specs, out_specs=out_specs, check_vma=False
    )
```

time: 228 us -> 47 us (0.21)
  other arithmetic: 108 us -> 0.01 us
  waiting for transfers between devices: 68.4 us -> 0.01 us
  local copies, waits for them, and re-layouts: 25.5 us -> 6.11 us
  Pallas kernels: 0 us -> 9.39 us
  starting transfers between devices: 22.1 us -> 30.5 us
    all_to_all x5 -> x0, waiting for transfers between devices: 68.4 us -> none  [the longest x1 41.6 us: on_device(): lax.all_to_all(send_taps, 'length', split_axis=0, concat_axis=0, tiled=True)]
    reduce_sum x69 -> x0, other arithmetic: 44.3 us -> none  [the longest x36 22.3 us: message(): summed = summed + (tap_weights[tap_index] * inside)[None, :] * shifted]
    ppermute x0 -> x3, starting transfers between devices: none -> 30.5 us  [on_device(): lax.ppermute(rows[k], 'length', [(i, (i + k) % ranks) for i in range(rank...]
    all_to_all x5 -> x0, starting transfers between devices: 22.1 us -> none  [the longest x1 6.32 us: on_device(): lax.all_to_all(note_slot.astype(jnp.bfloat16), 'length', split_axis=0, co...]
    dynamic_update_slice x6 -> x0, other arithmetic: 19.4 us -> none  [batched(): losses, slopes = lax.map(compute_block, shaped)]
    mul x66 -> x0, other arithmetic: 14.4 us -> none  [message(): summed = summed + (tap_weights[tap_index] * inside)[None, :] * shifted]
    gather x11 -> x0, local copies, waits for them, and re-layouts: 12.2 us -> none  [the longest x1 2.27 us: on_device(): jnp.take(returned, jnp.clip(buffer_place, 0, flag_count - 1), axis=0)]
    div x38 -> x0, other arithmetic: 9.47 us -> none  [the longest x30 6.05 us: normalize(): return raised / jnp.sum(raised, axis=0, keepdims=True)]
  transfers between devices with their start and end apart: 5 -> 3, of which waited for: 5 -> 0; matrix products, arithmetic and copies ran while one was open for 21% -> 0% of each run, Pallas kernels for 0% -> 15%
where the time goes in v2:
time: 47 us; the launch traced here: 46.7 us
  starting transfers between devices  30.5 us (65%)
  Pallas kernels  9.39 us (20%)
  local copies, waits for them, and re-layouts  6.11 us (13%)
  between operations  0.69 us (1%)
    ppermute x3, starting transfers between devices, on_device(): lax.ppermute(rows[k], 'length', [(i, (i + k) % ranks) for i in range(rank...  30.5 us
    pallas_call x2, Pallas kernels, process(): pl.pallas_call(functools.partial(tile_kernel, flagged, width, ranks), out...  9.39 us
    unnamed x20, local copies, waits for them, and re-layouts  5.6 us
  transfers between devices with their start and end apart: 3, of which 0 were waited for; matrix products, arithmetic and copies ran while one was open for 0% of the time, Pallas kernels for 15%

profile of v2, /device:TPU:0, one launch (start us, length us, event | category | flops | bytes accessed | tf_op | source)
XLA Modules:
  0.0 46.7 jit_solution(11111405489236034056)
XLA Ops:
  0.6 0.0 copy-start
  0.6 1.4 %copy-done = bf16[1,1,32,25,1024]{4,2,3,1,0:T(8,128)(2,1)S(1)} copy-done((bf16[1,1,32,25,1024]{4,2,3,1,0:T(8,128)(2,1)S(1)}, bf16[1,1,32,25,1024]{4,2,3,1,0:T(8,128)(2,1)}, u32[]{:S(2)}) %copy-start) | copy-done | bytes 1638424
  2.1 0.0 copy-start.1
  2.1 1.0 %copy-done.1 = bf16[1,1,32,8,1024]{4,3,2,1,0:T(8,128)(2,1)S(1)} copy-done((bf16[1,1,32,8,1024]{4,3,2,1,0:T(8,128)(2,1)S(1)}, bf16[1,1,32,8,1024]{4,3,2,1,0:T(8,128)(2,1)}, u32[]{:S(2)}) %copy-start.1) | copy-done | bytes 524312
  3.1 0.0 copy-start.3
  3.1 0.9 %copy-done.3 = s32[1,1,32,1024]{3,2,1,0:T(8,128)S(1)} copy-done((s32[1,1,32,1024]{3,2,1,0:T(8,128)S(1)}, s32[1,1,32,1024]{3,2,1,0:T(8,128)}, u32[]{:S(2)}) %copy-start.3) | copy-done | bytes 131096
  4.0 0.0 copy-start.4
  4.0 0.9 %copy-done.4 = s32[1,1,32,1024]{3,2,1,0:T(8,128)S(1)} copy-done((s32[1,1,32,1024]{3,2,1,0:T(8,128)S(1)}, s32[1,1,32,1024]{3,2,1,0:T(8,128)}, u32[]{:S(2)}) %copy-start.4) | copy-done | bytes 131096
  4.9 0.0 copy-start.8
  4.9 0.7 %copy-done.8 = s32[1,1,32]{2,1,0:T(1,128)S(1)} copy-done((s32[1,1,32]{2,1,0:T(1,128)S(1)}, s32[1,1,32]{2,1,0:T(1,128)}, u32[]{:S(2)}) %copy-start.8) | copy-done | bytes 152
  5.6 0.7 %copy-done.9 = s32[1,1,32]{2,1,0:T(1,128)S(1)} copy-done((s32[1,1,32]{2,1,0:T(1,128)S(1)}, s32[1,1,32]{2,1,0:T(1,128)}, u32[]{:S(2)}) %copy-start.9) | copy-done | bytes 152
  6.2 2.2 %flag_tiles.1 = (bf16[25,32,1024]{2,1,0:T(8,128)(2,1)}, f32[1,128]{1,0:T(1,128)S(1)}, f32[1,128]{1,0:T(1,128)S(1)}, f32[1,128]{1,0:T(1,128)S(1)}, f32[1,128]{1,0:T(1,128)S(1)}) custom-call(s32[32]{0:T(128)S(1)} %bitcast.31, s32[32]{0:T(128)S(1)} %bitcast.32, s32[1]{0:T(128)} %bitcast.2.refs_2_, bf16[25,32,1024]{2,1,0:T(8,128)(2,1)S(1)} %bitcast.23, ...), custom_call_target="tpu_custom_call" | custom-call | tf_op jit(solution)/shard_map/flag_tiles/pallas_call | solution.py:360
  8.5 15.5 %collective-permute-start = (f32[1,128]{1,0:T(1,128)S(1)}, f32[1,128]{1,0:T(1,128)S(1)}, u32[]{:S(2)}, u32[]{:S(2)}) collective-permute-start(f32[1,128]{1,0:T(1,128)S(1)} %get-tuple-element.10), channel_id=1, source_target_pairs={{0,4},{4,8},{8,12},{12,0},{1,5},{5,9},{9,13},{13,1},{2,6},{6,10},{... | collective-permute-start | bytes 1544 | tf_op jit(solution)/shard_map/ppermute | solution.py:420
  23.9 15.0 %collective-permute-start.1 = (f32[1,128]{1,0:T(1,128)S(1)}, f32[1,128]{1,0:T(1,128)S(1)}, u32[]{:S(2)}, u32[]{:S(2)}) collective-permute-start(f32[1,128]{1,0:T(1,128)S(1)} %get-tuple-element.11), channel_id=1, source_target_pairs={{0,8},{4,12},{8,0},{12,4},{1,9},{5,13},{9,1},{13,5},{2,10},{6,14},... | collective-permute-start | bytes 1544 | tf_op jit(solution)/shard_map/ppermute | solution.py:420
  39.0 0.0 collective-permute-start.2
  39.0 0.0 copy-done.2
  39.0 0.0 copy-done.5
  39.0 0.0 copy-done.6
  39.0 0.0 copy-done.7
  39.0 7.2 %res_tiles.1 = bf16[25,8,1024]{2,1,0:T(8,128)(2,1)} custom-call(bf16[25,8,1024]{2,1,0:T(8,128)(2,1)S(1)} %bitcast.25, bf16[8,8,1024]{2,1,0:T(8,128)(2,1)S(1)} %bitcast.28, s32[8,1024]{1,0:T(8,128)S(1)} %bitcast.29, s32[8,1024]{1,0:T(8,128)S(1)} %bitcast.30), custom_call_target="tpu_custom_call" | custom-call | tf_op jit(solution)/shard_map/res_tiles/pallas_call | solution.py:360
  46.2 0.0 collective-permute-done
  46.2 0.0 collective-permute-done.1
  46.2 0.0 collective-permute-done.2
  46.2 0.5 %slice_bitcast_fusion = f32[1,1,16]{2,1,0:T(1,128)} fusion(f32[1,128]{1,0:T(1,128)S(1)} %add_add_fusion), kind=kLoop, calls=%fused_computation | loop fusion | bytes 128 | tf_op jit(solution)/shard_map/broadcast_in_dim | solution.py:427
  (6 shorter events, 0.0 us)
Async XLA Ops:
  0.6 1.4 %copy-start = (bf16[1,1,32,25,1024]{4,2,3,1,0:T(8,128)(2,1)S(1)}, bf16[1,1,32,25,1024]{4,2,3,1,0:T(8,128)(2,1)}, u32[]{:S(2)}) copy-start(bf16[1,1,32,25,1024]{4,2,3,1,0:T(8,128)(2,1)} %param.10) | copy-start | bytes 4915204
  2.1 1.0 %copy-start.1 = (bf16[1,1,32,8,1024]{4,3,2,1,0:T(8,128)(2,1)S(1)}, bf16[1,1,32,8,1024]{4,3,2,1,0:T(8,128)(2,1)}, u32[]{:S(2)}) copy-start(bf16[1,1,32,8,1024]{4,3,2,1,0:T(8,128)(2,1)} %param.11) | copy-start | bytes 1572868
  3.1 0.9 %copy-start.3 = (s32[1,1,32,1024]{3,2,1,0:T(8,128)S(1)}, s32[1,1,32,1024]{3,2,1,0:T(8,128)}, u32[]{:S(2)}) copy-start(s32[1,1,32,1024]{3,2,1,0:T(8,128)} %param.12) | copy-start | bytes 393220
  4.0 0.9 %copy-start.4 = (s32[1,1,32,1024]{3,2,1,0:T(8,128)S(1)}, s32[1,1,32,1024]{3,2,1,0:T(8,128)}, u32[]{:S(2)}) copy-start(s32[1,1,32,1024]{3,2,1,0:T(8,128)} %param.13) | copy-start | bytes 393220
  4.9 0.7 %copy-start.8 = (s32[1,1,32]{2,1,0:T(1,128)S(1)}, s32[1,1,32]{2,1,0:T(1,128)}, u32[]{:S(2)}) copy-start(s32[1,1,32]{2,1,0:T(1,128)} %param.14) | copy-start | bytes 388
  5.6 0.7 %copy-start.9 = (s32[1,1,32]{2,1,0:T(1,128)S(1)}, s32[1,1,32]{2,1,0:T(1,128)}, u32[]{:S(2)}) copy-start(s32[1,1,32]{2,1,0:T(1,128)} %param.15) | copy-start | bytes 388
  6.2 32.8 %copy-start.2 = (bf16[1,1,8,25,1024]{4,2,3,1,0:T(8,128)(2,1)S(1)}, bf16[1,1,8,25,1024]{4,2,3,1,0:T(8,128)(2,1)}, u32[]{:S(2)}) copy-start(bf16[1,1,8,25,1024]{4,2,3,1,0:T(8,128)(2,1)} %param.16) | copy-start | bytes 1228804
  6.2 32.8 %copy-start.5 = (bf16[1,1,8,8,1024]{4,3,2,1,0:T(8,128)(2,1)S(1)}, bf16[1,1,8,8,1024]{4,3,2,1,0:T(8,128)(2,1)}, u32[]{:S(2)}) copy-start(bf16[1,1,8,8,1024]{4,3,2,1,0:T(8,128)(2,1)} %param.17) | copy-start | bytes 393220
  6.2 32.8 %copy-start.6 = (s32[1,1,8,1024]{3,2,1,0:T(8,128)S(1)}, s32[1,1,8,1024]{3,2,1,0:T(8,128)}, u32[]{:S(2)}) copy-start(s32[1,1,8,1024]{3,2,1,0:T(8,128)} %param.18) | copy-start | bytes 98308
  6.2 32.8 %copy-start.7 = (s32[1,1,8,1024]{3,2,1,0:T(8,128)S(1)}, s32[1,1,8,1024]{3,2,1,0:T(8,128)}, u32[]{:S(2)}) copy-start(s32[1,1,8,1024]{3,2,1,0:T(8,128)} %param.19) | copy-start | bytes 98308
  8.5 37.7 %collective-permute-start = (f32[1,128]{1,0:T(1,128)S(1)}, f32[1,128]{1,0:T(1,128)S(1)}, u32[]{:S(2)}, u32[]{:S(2)}) collective-permute-start(f32[1,128]{1,0:T(1,128)S(1)} %get-tuple-element.10), channel_id=1, source_target_pairs={{0,4},{4,8},{8,12},{12,0},{1,5},{5,9},{9,13},{13,1},{2,6},{6,10},{... | collective-permute-start | bytes 1544 | tf_op jit(solution)/shard_map/ppermute | solution.py:420
  23.9 22.3 %collective-permute-start.1 = (f32[1,128]{1,0:T(1,128)S(1)}, f32[1,128]{1,0:T(1,128)S(1)}, u32[]{:S(2)}, u32[]{:S(2)}) collective-permute-start(f32[1,128]{1,0:T(1,128)S(1)} %get-tuple-element.11), channel_id=1, source_target_pairs={{0,8},{4,12},{8,0},{12,4},{1,9},{5,13},{9,1},{13,5},{2,10},{6,14},... | collective-permute-start | bytes 1544 | tf_op jit(solution)/shard_map/ppermute | solution.py:420
  39.0 7.2 %collective-permute-start.2 = (f32[1,128]{1,0:T(1,128)S(1)}, f32[1,128]{1,0:T(1,128)S(1)}, u32[]{:S(2)}, u32[]{:S(2)}) collective-permute-start(f32[1,128]{1,0:T(1,128)S(1)} %get-tuple-element.12), channel_id=1, source_target_pairs={{0,12},{4,0},{8,4},{12,8},{1,13},{5,1},{9,5},{13,9},{2,14},{6,2},{... | collective-permute-start | bytes 1544 | tf_op jit(solution)/shard_map/ppermute | solution.py:420

commit v3 on v2

v3 whole, which is shorter than its diff:
```python
import functools

import jax
import jax.numpy as jnp
from jax import lax
from jax.experimental import pallas as pl
from jax.experimental.pallas import tpu as pltpu
from jax.sharding import PartitionSpec as P

CLASSES = 8
DIFFS = CLASSES - 1
TAPS = 25
TILE = 32
ITERS = 3
RECV = 16
LANES = 128
BLOCKS = 4
PIXELS = TILE * TILE
PAIR = 2 * DIFFS * 8
SCORES = (CLASSES + 2) * 8
F32 = jnp.float32
BF16 = jnp.bfloat16


def dot(left, right):
    return jnp.dot(left, right, preferred_element_type=F32)


def tile_kernel(flagged, width, ranks, *refs):
    if flagged:
        dest_ref, slot_ref, me_ref, *refs = refs
    k_refs, refs = refs[:5], refs[5:]
    u_ref, lab_ref, msk_ref, out_ref, *refs = refs
    if flagged:
        loss_refs, refs = refs[:ranks], refs[ranks:]
    swap, move, down, up, kx, kt, uu, ux, ud, acc, hl, fields, beliefs, grads, sums = refs
    block = pl.program_id(0)
    teams = width // 8
    cuts = BLOCKS // teams
    rows = TILE // cuts
    quads = rows // 4
    field = rows // 2 * PAIR
    haloed = field + 2 * PAIR
    spread = 5 * haloed

    @pl.when(block == 0)
    def _():
        row = lax.broadcasted_iota(jnp.int32, (LANES, LANES), 0)
        lane = lax.broadcasted_iota(jnp.int32, (LANES, LANES), 1)
        same = row % TILE == lane % TILE
        for j in range(BLOCKS):
            for r in range(BLOCKS):
                hit = same & (row // TILE == r) & (lane // TILE == j)
                swap[pl.ds(j * LANES, LANES), pl.ds(r * LANES, LANES)] = jnp.where(
                    hit, 1.0, 0.0
                ).astype(BF16)
        for b in range(5):
            seen = lane % TILE + b - 2
            inside = (seen >= 0) & (seen < TILE)
            cut = lane // TILE % cuts
            for ref, jump in ((move, 0), (down, -TILE), (up, TILE)):
                place = b
                if jump == 0:
                    if b == 2:
                        continue
                    place = b - (b > 2)
                hit = inside & (row == lane + b - 2 + jump)
                if jump:
                    hit = hit & (cut > 0 if jump < 0 else cut < cuts - 1)
                part = jnp.where(hit, 1.0, 0.0).astype(BF16)
                for twice in range(2):
                    ref[pl.ds(twice * LANES, LANES), pl.ds(place * LANES, LANES)] = part
        for ref in (down, up):
            ref[:, pl.ds(5 * LANES, LANES)] = jnp.zeros((2 * LANES, LANES), BF16)
        uu[...] = jnp.zeros_like(uu)
        if flagged:
            sums[...] = jnp.zeros_like(sums)

    if flagged:
        live = jnp.int32(0)
        for j in range(sums.shape[0]):
            live = live + (dest_ref[j] >= 0).astype(jnp.int32)
    else:
        live = jnp.int32(width)

    def kernel_at(t, r):
        return ((r % 4) * quads + r // 4) * TAPS + t

    def field_at(slot, b, r, c):
        place = b * haloed + ((r + 2) // 2) * PAIR + c * 16 + (r % 2) * 8
        return slot * spread + place

    def plain_at(r, c):
        return ((r // 2) * DIFFS + c) * 16 + (r % 2) * 8

    def eight(start):
        return pl.ds(pl.multiple_of(start, 8), 8)

    def sixteen(start):
        return pl.ds(pl.multiple_of(start, 16), 16)

    def swapped(left):
        for two in range(BLOCKS // 2):
            got = dot(left, swap[:, pl.ds(two * 2 * LANES, 2 * LANES)])
            yield 2 * two, got[:, :LANES]
            yield 2 * two + 1, got[:, LANES:]

    def bring_kernels():
        for m in range(quads):
            parts = []
            for j in range(BLOCKS):
                team, cut = divmod(j, cuts)
                lanes = pl.ds((m + quads * cut) * LANES, LANES)
                part = jnp.concatenate([ref[:, :, lanes] for ref in k_refs], axis=0)
                part = part.astype(F32)[:, 8 * team : 8 * team + 8]
                parts.append(part.reshape(TAPS * 8, LANES).astype(BF16))
            for r, got in swapped(jnp.concatenate(parts, axis=1)):
                kx[pl.ds((r * quads + m) * TAPS, TAPS), :, :] = got.reshape(
                    TAPS, 8, LANES
                )

    def give_kernels():
        for m in range(quads):
            left = jnp.concatenate(
                [
                    kx[pl.ds((r * quads + m) * TAPS, TAPS), :, :]
                    .reshape(TAPS * 8, LANES)
                    .astype(BF16)
                    for r in range(BLOCKS)
                ],
                axis=1,
            )
            got = {j: part.reshape(TAPS, 8, LANES) for j, part in swapped(left)}
            for cut in range(cuts):
                part = [got[team * cuts + cut] for team in range(teams)]
                lanes = pl.ds((m + quads * cut) * LANES, LANES)
                out_ref[:, :, lanes] = jnp.concatenate(part, axis=1).astype(BF16)

    def emit(slot, pair, c, value):
        fields[sixteen(field_at(slot, 2, 2 * pair, c)), :] = value
        high = value.astype(BF16)
        low = (value - high.astype(F32)).astype(BF16)
        place = pl.ds(plain_at(2 * pair, c), 16)
        hl[place, pl.ds(0, LANES)] = high
        hl[place, pl.ds(LANES, LANES)] = low

    def shift(slot):
        def put(pair, source, matrix, names):
            got = dot(hl[source, :], matrix)
            for n, b in enumerate(names):
                start = field_at(slot, b, 2 * pair, 0)
                fields[pl.ds(pl.multiple_of(start, 16), source.size), :] = got[
                    :, n * LANES : (n + 1) * LANES
                ]

        first, last = pl.ds(0, PAIR), pl.ds(field - PAIR, PAIR)
        for two, names in enumerate(((2, 3), (0, 1), (4,))):
            lanes = pl.ds(names[0] * LANES, 2 * LANES)
            put(-1, last, down[:, lanes], names)
            put(rows // 2, first, up[:, lanes], names)
            if two == 0:
                put(0, pl.ds(0, field), move[:, pl.ds(0, 2 * LANES)], (0, 1))
            elif two == 1:
                put(0, pl.ds(0, field), move[:, pl.ds(2 * LANES, 2 * LANES)], (3, 4))

    def message(taps_ref, slot, start_ref):
        for b in (2, 0, 1, 3, 4):
            for quad in range(quads):
                taps = [
                    [taps_ref[kernel_at(5 * a + b, 4 * quad + r)] for r in range(4)]
                    for a in range(5)
                ]
                for c in range(DIFFS):
                    near = [
                        fields[eight(field_at(slot, b, 4 * quad + r - 2, c)), :]
                        for r in range(8)
                    ]
                    for r in range(4):
                        place = pl.ds(plain_at(4 * quad + r, c), 8)
                        if b == 2:
                            total = None if start_ref is None else start_ref[place, :]
                        else:
                            total = acc[place, :]
                        for a in range(5):
                            term = taps[a][r] * near[r + a]
                            total = term if total is None else total + term
                        acc[place, :] = total

    def work():
        for a in range(5):
            for b in range(5):
                for r in range(rows):
                    source = r - (a - 2)
                    turn = b - 2
                    if source < 0:
                        source, turn = source + rows, turn + TILE
                    elif source >= rows:
                        source, turn = source - rows, turn - TILE
                    value = kx[kernel_at(5 * a + b, source)]
                    if turn:
                        value = pltpu.roll(value, turn % LANES, 1)
                    kt[kernel_at(5 * (4 - a) + 4 - b, r)] = value

        index = lax.broadcasted_iota(jnp.int32, (8, LANES), 0) + block * width
        for team in range(teams):
            mine = pl.ds(8 * team, 8)
            for s in range(8):
                cut = pl.ds(s * LANES, LANES)
                for i in range(8):
                    uu[team, pl.ds(s * SCORES + i, CLASSES, stride=8), :] = u_ref[
                        8 * team + i, :, cut
                    ].astype(F32)
                target = jnp.where(
                    (index + 8 * team < live) & (msk_ref[mine, cut] == 1),
                    lab_ref[mine, cut],
                    CLASSES,
                )
                uu[team, pl.ds(s * SCORES + 8 * CLASSES, 8), :] = target.astype(F32)
        left = jnp.concatenate(
            [
                jnp.concatenate(
                    [
                        uu[
                            j // cuts, pl.ds((m + quads * (j % cuts)) * SCORES, SCORES), :
                        ].astype(BF16)
                        for j in range(BLOCKS)
                    ],
                    axis=1,
                )
                for m in range(quads)
            ],
            axis=0,
        )
        for r, got in swapped(left):
            ux[pl.ds(r * quads * SCORES, quads * SCORES), :] = got

        def score(r, f):
            return ux[pl.ds(((r % 4) * quads + r // 4) * SCORES + 8 * f, 8), :]

        for r in range(rows):
            last = score(r, CLASSES - 1)
            for c in range(DIFFS):
                value = score(r, c) - last
                ud[pl.ds(plain_at(r, c), 8), :] = value
                acc[pl.ds(plain_at(r, c), 8), :] = value

        def forward(it, carry):
            for pair in range(rows // 2):
                at = lambda c: pl.ds(plain_at(2 * pair, c), 16)
                raised = [jnp.exp(acc[at(c), :]) for c in range(DIFFS)]
                inverse = 1.0 / (functools.reduce(jnp.add, raised) + 1.0)
                for c in range(DIFFS):
                    belief = raised[c] * inverse
                    beliefs[sixteen(it * field + plain_at(2 * pair, c)), :] = belief
                    emit(it, pair, c, belief - inverse)
            shift(it)
            message(kx, it, ud)
            return carry

        lax.fori_loop(0, ITERS, forward, 0)

        lost = jnp.zeros((8, LANES), F32)
        for r in range(rows):
            label = score(r, CLASSES)
            diffs = [acc[pl.ds(plain_at(r, c), 8), :] for c in range(DIFFS)]
            raised = [jnp.exp(d) for d in diffs]
            total = functools.reduce(jnp.add, raised) + 1.0
            inverse = 1.0 / total
            used = label < CLASSES
            chosen = jnp.zeros((8, LANES), F32)
            for c in range(DIFFS):
                hit = label == c
                chosen = jnp.where(hit, diffs[c], chosen)
                slope = raised[c] * inverse - jnp.where(hit, 1.0, 0.0)
                grads[pl.ds((ITERS - 1) * field + plain_at(r, c), 8), :] = jnp.where(
                    used, slope, 0.0
                )
            lost = lost + jnp.where(used, jnp.log(total) - chosen, 0.0)
        if flagged:
            lane = lax.broadcasted_iota(jnp.int32, (8, LANES), 1)
            for team in range(teams):
                one = jnp.where(lane // (cuts * TILE) == team, lost, 0.0)
                one = jnp.sum(one, axis=1, keepdims=True) * (1.0 / TILE)
                sums[eight(block * width + 8 * team), :] = jnp.broadcast_to(one, (8, LANES))

        def backward(step, carry):
            it = ITERS - 1 - step
            for pair in range(rows // 2):
                for c in range(DIFFS):
                    place = plain_at(2 * pair, c)
                    emit(ITERS, pair, c, grads[sixteen(it * field + place), :])
            shift(ITERS)
            message(kt, ITERS, None)
            for pair in range(rows // 2):
                at = lambda c: plain_at(2 * pair, c)
                back = [acc[pl.ds(at(c), 16), :] for c in range(DIFFS)]
                mean = functools.reduce(
                    jnp.add,
                    [
                        back[c] * fields[sixteen(field_at(it, 2, 2 * pair, c)), :]
                        for c in range(DIFFS)
                    ],
                )
                for c in range(DIFFS):
                    belief = beliefs[sixteen(it * field + at(c)), :]
                    grads[sixteen((it - 1) * field + at(c)), :] = belief * (back[c] - mean)
            return carry

        lax.fori_loop(0, ITERS - 1, backward, 0)

        def gather(b, carry):
            for quad in range(quads):
                totals = [[None] * 4 for _ in range(5)]
                for it in range(ITERS):
                    for c in range(DIFFS):
                        near = [
                            fields[eight(field_at(it, b, 4 * quad + r - 2, c)), :]
                            for r in range(8)
                        ]
                        for r in range(4):
                            slope = grads[
                                pl.ds(it * field + plain_at(4 * quad + r, c), 8), :
                            ]
                            for a in range(5):
                                term = slope * near[r + a]
                                old = totals[a][r]
                                totals[a][r] = term if old is None else old + term
                for a in range(5):
                    for r in range(4):
                        kx[kernel_at(5 * a + b, 4 * quad + r)] = totals[a][r]
            return carry

        lax.fori_loop(0, 5, gather, 0)

    @pl.when(live > block * width)
    def _():
        bring_kernels()
        work()
        give_kernels()

    if not flagged:
        return

    @pl.when(live <= block * width)
    def _():
        out_ref[...] = jnp.zeros_like(out_ref)

    @pl.when(block == pl.num_programs(0) - 1)
    def _():
        high = -(-ranks // 8) * 8
        spot = lax.broadcasted_iota(
            jnp.int32, (high, LANES), 0
        ) * LANES + lax.broadcasted_iota(jnp.int32, (high, LANES), 1)
        placed = jnp.zeros((high, LANES), F32)
        for j in range(sums.shape[0]):
            far = dest_ref[j] - me_ref[0]
            far = jnp.where(far < 0, far + ranks, far)
            here = jnp.where(dest_ref[j] >= 0, far * LANES + slot_ref[j], -1)
            placed = jnp.where(spot == here, sums[pl.ds(j, 1), :], placed)
        for k, ref in enumerate(loss_refs):
            ref[...] = placed[k : k + 1, :]


def process(kernels, unary, labels, mask, lists, ranks):
    kernels = jnp.transpose(kernels, (1, 0, 2))
    count = kernels.shape[1]
    flagged = lists is not None
    width = 16 if count % 16 == 0 else 8
    rows = TILE * width // (8 * BLOCKS)
    field = rows // 2 * PAIR
    haloed = field + 2 * PAIR

    out_shape = [jax.ShapeDtypeStruct(kernels.shape, BF16)]
    out_specs = [pl.BlockSpec((TAPS, width, PIXELS), lambda g, *_: (0, g, 0))]
    if flagged:
        out_shape += [jax.ShapeDtypeStruct((1, LANES), F32)] * ranks
        out_specs += [pl.BlockSpec((1, LANES), lambda g, *_: (0, 0))] * ranks
    grads, *rows = pl.pallas_call(
        functools.partial(tile_kernel, flagged, width, ranks),
        out_shape=out_shape,
        grid_spec=pltpu.PrefetchScalarGridSpec(
            num_scalar_prefetch=3 if flagged else 0,
            grid=(count // width,),
            in_specs=[
                *[
                    pl.BlockSpec((5, width, PIXELS), lambda g, *_, a=a: (a, g, 0))
                    for a in range(5)
                ],
                pl.BlockSpec((width, CLASSES, PIXELS), lambda g, *_: (g, 0, 0)),
                pl.BlockSpec((width, PIXELS), lambda g, *_: (g, 0)),
                pl.BlockSpec((width, PIXELS), lambda g, *_: (g, 0)),
            ],
            out_specs=out_specs,
            scratch_shapes=[
                pltpu.VMEM((BLOCKS * LANES, BLOCKS * LANES), BF16),
                pltpu.VMEM((2 * LANES, 4 * LANES), BF16),
                pltpu.VMEM((2 * LANES, 6 * LANES), BF16),
                pltpu.VMEM((2 * LANES, 6 * LANES), BF16),
                pltpu.VMEM((rows * TAPS, 8, LANES), F32),
                pltpu.VMEM((rows * TAPS, 8, LANES), F32),
                pltpu.VMEM((width // 8, 8 * SCORES, LANES), F32),
                pltpu.VMEM((rows * SCORES, LANES), F32),
                pltpu.VMEM((field, LANES), F32),
                pltpu.VMEM((field, LANES), F32),
                pltpu.VMEM((field, 2 * LANES), BF16),
                pltpu.VMEM(((ITERS + 1) * 5 * haloed, LANES), F32),
                pltpu.VMEM((ITERS * field, LANES), F32),
                pltpu.VMEM((ITERS * field, LANES), F32),
                pltpu.VMEM((count, LANES), F32),
            ],
        ),
        compiler_params=pltpu.CompilerParams(vmem_limit_bytes=58 * 1024 * 1024),
        name="flag_tiles" if flagged else "res_tiles",
    )(*(lists if flagged else ()), *[kernels] * 5, unary, labels, mask)
    return jnp.transpose(grads, (1, 0, 2)), rows


def on_device(
    flag_kernels,
    flag_unary,
    flag_labels,
    flag_mask,
    dest_list,
    slot_list,
    res_kernels,
    res_unary,
    res_labels,
    res_mask,
):
    ranks = lax.axis_size("length")
    me = lax.axis_index("length").astype(jnp.int32).reshape(1)
    flag_grad, rows = process(
        flag_kernels[0, 0],
        flag_unary[0, 0],
        flag_labels[0, 0],
        flag_mask[0, 0],
        (dest_list[0, 0], slot_list[0, 0], me),
        ranks,
    )
    got = [rows[0]] + [
        lax.ppermute(rows[k], "length", [(i, (i + k) % ranks) for i in range(ranks)])
        for k in range(1, ranks)
    ]
    res_grad, _ = process(
        res_kernels[0, 0], res_unary[0, 0], res_labels[0, 0], res_mask[0, 0], None, ranks
    )
    helper_loss = functools.reduce(jnp.add, got)[:, :RECV]
    return flag_grad[None, None], res_grad[None, None], helper_loss[None]


def solution(mesh):
    tiles = ("groups", "sector", "pair")
    spec = lambda extra: P("length", tiles, *([None] * extra))
    in_specs = tuple(spec(n) for n in (3, 3, 2, 2, 1, 1, 3, 3, 2, 2))
    out_specs = tuple(spec(n) for n in (3, 3, 1))
    return jax.shard_map(
        on_device, mesh=mesh, in_specs=in_specs, out_specs=out_specs, check_vma=False
    )
```

time: 47 us -> 38.5 us (0.82); the launches traced: 46.7 us -> 39 us
  local copies, waits for them, and re-layouts: 6.11 us -> 0.52 us
  starting transfers between devices: 30.5 us -> 26.7 us
  Pallas kernels: 9.39 us -> 11.1 us
    unnamed x20 -> x2, local copies, waits for them, and re-layouts: 5.6 us -> 0.01 us
    ppermute x3, starting transfers between devices: 30.5 us -> 26.7 us  [on_device(): lax.ppermute(rows[k], 'length', [(i, (i + k) % ranks) for i in range(rank...]
    pallas_call x2, Pallas kernels: 9.39 us -> 11.1 us  [process(): pl.pallas_call(functools.partial(tile_kernel, flagged, width, ranks), out...]
  transfers between devices with their start and end apart: 3 -> 3, of which waited for: 0 -> 0; matrix products, arithmetic and copies ran while one was open for 0% -> 0% of each run, Pallas kernels for 15% -> 19%
where the time goes in v3:
time: 38.5 us; the launch traced here: 39 us
  starting transfers between devices  26.7 us (69%)
  Pallas kernels  11.1 us (29%)
  between operations  0.67 us (2%)
  local copies, waits for them, and re-layouts  0.52 us (1%)
    ppermute x3, starting transfers between devices, on_device(): lax.ppermute(rows[k], 'length', [(i, (i + k) % ranks) for i in range(rank...  26.7 us
    pallas_call x2, Pallas kernels, process(): pl.pallas_call(functools.partial(tile_kernel, flagged, width, ranks), out...  11.1 us
  transfers between devices with their start and end apart: 3, of which 0 were waited for; matrix products, arithmetic and copies ran while one was open for 0% of the time, Pallas kernels for 19%

profile of v3, /device:TPU:0, one launch (start us, length us, event | category | flops | bytes accessed | tf_op | source)
XLA Modules:
  0.0 39.0 jit_solution(555736137852883445)
XLA Ops:
  0.6 3.6 %flag_tiles.1 = (bf16[25,32,1024]{2,1,0:T(8,128)(2,1)}, f32[1,128]{1,0:T(1,128)}, f32[1,128]{1,0:T(1,128)}, f32[1,128]{1,0:T(1,128)}, f32[1,128]{1,0:T(1,128)}) custom-call(s32[32]{0:T(128)} %bitcast.40, s32[32]{0:T(128)} %bitcast.41, s32[1]{0:T(128)} %bitcast.2.refs_2_, bf16[25,32,1024]{2,1,0:T(8,128)(2,1)} %bitcast.23, bf16[25,32,1024]{2,1,0:T(8,128)(2,1)} %bitcast.24, ...), custom_call_target="tpu_custom_call" | custom-call | tf_op jit(solution)/shard_map/flag_tiles/pallas_call | solution.py:378
  4.2 0.0 copy-start
  4.2 22.8 %collective-permute-start = (f32[1,128]{1,0:T(1,128)}, f32[1,128]{1,0:T(1,128)S(1)}, u32[]{:S(2)}, u32[]{:S(2)}) collective-permute-start(f32[1,128]{1,0:T(1,128)} %get-tuple-element.10), channel_id=1, source_target_pairs={{0,4},{4,8},{8,12},{12,0},{1,5},{5,9},{9,13},{13,1},{2,6},{6,10},{... | collective-permute-start | bytes 1544 | tf_op jit(solution)/shard_map/ppermute | solution.py:441
  27.1 1.1 %collective-permute-start.1 = (f32[1,128]{1,0:T(1,128)}, f32[1,128]{1,0:T(1,128)S(1)}, u32[]{:S(2)}, u32[]{:S(2)}) collective-permute-start(f32[1,128]{1,0:T(1,128)} %get-tuple-element.11), channel_id=1, source_target_pairs={{0,8},{4,12},{8,0},{12,4},{1,9},{5,13},{9,1},{13,5},{2,10},{6,14},... | collective-permute-start | bytes 1544 | tf_op jit(solution)/shard_map/ppermute | solution.py:441
  28.1 2.8 %collective-permute-start.2 = (f32[1,128]{1,0:T(1,128)}, f32[1,128]{1,0:T(1,128)S(1)}, u32[]{:S(2)}, u32[]{:S(2)}) collective-permute-start(f32[1,128]{1,0:T(1,128)} %get-tuple-element.12), channel_id=1, source_target_pairs={{0,12},{4,0},{8,4},{12,8},{1,13},{5,1},{9,5},{13,9},{2,14},{6,2},{... | collective-permute-start | bytes 1544 | tf_op jit(solution)/shard_map/ppermute | solution.py:441
  31.0 7.4 %res_tiles.1 = bf16[25,8,1024]{2,1,0:T(8,128)(2,1)} custom-call(bf16[25,8,1024]{2,1,0:T(8,128)(2,1)} %bitcast.28, bf16[25,8,1024]{2,1,0:T(8,128)(2,1)} %bitcast.29, bf16[25,8,1024]{2,1,0:T(8,128)(2,1)} %bitcast.30, bf16[25,8,1024]{2,1,0:T(8,128)(2,1)} %bitcast.31, bf16[25,8,1024]{2,1,0:T(8,128)(2,1)} %bitcast.32, bf16[8,8,1024]{2,1,0:T(8,128)(2,1)} %bitcast.37, ...), custom_call_target="tpu_custom_call" | custom-call | tf_op jit(solution)/shard_map/res_tiles/pallas_call | solution.py:378
  38.4 0.0 collective-permute-done
  38.4 0.0 collective-permute-done.1
  38.4 0.0 collective-permute-done.2
  38.5 0.0 copy-done
  38.5 0.5 %slice_bitcast_fusion = f32[1,1,16]{2,1,0:T(1,128)} fusion(f32[1,128]{1,0:T(1,128)S(1)} %add_add_fusion), kind=kLoop, calls=%fused_computation | loop fusion | bytes 128 | tf_op jit(solution)/shard_map/broadcast_in_dim | solution.py:448
  (1 shorter events, 0.0 us)
Async XLA Ops:
  4.2 34.2 %copy-start = (f32[1,128]{1,0:T(1,128)S(1)}, f32[1,128]{1,0:T(1,128)}, u32[]{:S(2)}) copy-start(f32[1,128]{1,0:T(1,128)} %get-tuple-element.9) | copy-start | bytes 1540
  4.2 34.2 %collective-permute-start = (f32[1,128]{1,0:T(1,128)}, f32[1,128]{1,0:T(1,128)S(1)}, u32[]{:S(2)}, u32[]{:S(2)}) collective-permute-start(f32[1,128]{1,0:T(1,128)} %get-tuple-element.10), channel_id=1, source_target_pairs={{0,4},{4,8},{8,12},{12,0},{1,5},{5,9},{9,13},{13,1},{2,6},{6,10},{... | collective-permute-start | bytes 1544 | tf_op jit(solution)/shard_map/ppermute | solution.py:441
  27.1 11.4 %collective-permute-start.1 = (f32[1,128]{1,0:T(1,128)}, f32[1,128]{1,0:T(1,128)S(1)}, u32[]{:S(2)}, u32[]{:S(2)}) collective-permute-start(f32[1,128]{1,0:T(1,128)} %get-tuple-element.11), channel_id=1, source_target_pairs={{0,8},{4,12},{8,0},{12,4},{1,9},{5,13},{9,1},{13,5},{2,10},{6,14},... | collective-permute-start | bytes 1544 | tf_op jit(solution)/shard_map/ppermute | solution.py:441
  28.1 10.3 %collective-permute-start.2 = (f32[1,128]{1,0:T(1,128)}, f32[1,128]{1,0:T(1,128)S(1)}, u32[]{:S(2)}, u32[]{:S(2)}) collective-permute-start(f32[1,128]{1,0:T(1,128)} %get-tuple-element.12), channel_id=1, source_target_pairs={{0,12},{4,0},{8,4},{12,8},{1,13},{5,1},{9,5},{13,9},{2,14},{6,2},{... | collective-permute-start | bytes 1544 | tf_op jit(solution)/shard_map/ppermute | solution.py:441
